TPU v7x, 128 devices: a whole 4x4x4 slice. The times are simulated.
128 devices in a mesh: section: 4 (over x), dp: 32 (over y, z, core).
Axes of the slice: x: 4, y: 4, z: 4, core: 2. Of those that a mesh axis runs over, the one named last changes fastest.
Arguments:
- embeddings: bfloat16 [8192, 1024], P('dp'), may hold values from -6 to 6
- in_proj: bfloat16 [4, 1024, 2048], P('section'), may hold values from -0.1875 to 0.1875
- out_proj: bfloat16 [4, 1024, 512], P('section'), may hold values from -0.25 to 0.25
- hist_cache: bfloat16 [4, 512, 128, 1024], P('section', 'dp'), may hold values from -6 to 6
- hist_len: int32 [64], P('dp'), may hold values from 1 to 2048, 98304 in all
- block_mask: int32 [64, 16], P('dp'), may hold values 0 or 1
- block_owner: int32 [64, 16, 1], P('dp'), may hold values from 0 to 31; in each aligned block of 32 rows (0 to 31, 32 to 63, ..., all dimensions but the last counted through in order) at most 2 rows name the same one
- block_slot: int32 [64, 16], P('dp'), may hold values from 0 to 15
- cotangent: bfloat16 [8192, 1024], P('dp'), may hold values from -1.5 to 1.5
Outputs:
- layer_outputs: bfloat16 [4, 8192, 1024], P('section', 'dp')
- input_grads: bfloat16 [4, 8192, 1024], P('section', 'dp')
- grad_in_proj: float32 [4, 1024, 2048], P('section', 'dp')
- grad_out_proj: float32 [4, 1024, 512], P('section', 'dp')
Inputs may be any that keep to these rules, and one draw needn't show every extreme that they name: `hist_len`: some user has exactly 2048 history events. `block_owner`: among the blocks listed for the users of one dp index, at most 2 lie on any one owner, and in every draw some owner holds exactly 2 of them.
All inputs are finite; a program needn't handle non-finite values. No bound on the sum of `hist_len` or of `block_mask` on one device may be relied on, other than what follows from the above.
Results may differ from a plain program's by a relative error of at most 0.035.
Values may be sent and summed in bfloat16 or wider, within the bound.
A program may use at most 320 MiB of HBM per device.

v0:
```python
from functools import partial
import math

import jax
import jax.numpy as jnp
from jax import lax
from jax.sharding import PartitionSpec as P

HEADS = 4
EVT = 128
HBLK = 16


epsilon = 1e-06
group_blocks = 4


def passed_along(array, axis, by):
    peers = lax.axis_size(axis)
    pairs = [(i, i + by) for i in range(peers) if 0 <= i + by < peers]
    return lax.ppermute(array, axis, pairs)


def norm_rows(values):
    row_mean = jnp.mean(values, axis=-1, keepdims=True)
    centred = values - row_mean
    return centred * lax.rsqrt(jnp.mean(centred * centred, axis=-1, keepdims=True) + epsilon)


def event_mask(lengths, blocks):
    position = jnp.arange(HBLK * EVT, dtype=jnp.int32).reshape(HBLK, EVT)
    live_cells = (position[None, :, :] < lengths[:, None, None]) & (blocks[:, :, None] > 0)
    return live_cells.astype(jnp.float32)


def keep_float(values):
    return values


def attend(projected, history, key_mask, inv_count, converter):
    user_count = history.shape[0]
    width = projected.shape[1] // 4
    head_size = width // HEADS
    activated = jax.nn.silu(projected).astype(jnp.bfloat16)
    gate_units = activated[:, :width]
    own_value = activated[:, width : 2 * width]
    own_query = activated[:, 2 * width : 3 * width]
    own_key = activated[:, 3 * width :]
    events = own_query.shape[0] // user_count
    all_keys = jnp.concatenate(
        [history[:, :, :width], own_key.reshape(user_count, events, width)], axis=1
    )
    all_values = jnp.concatenate(
        [history[:, :, width:], own_value.reshape(user_count, events, width)], axis=1
    )
    causal = (jnp.arange(events)[None, :] <= jnp.arange(events)[:, None]).astype(jnp.float32)
    history_part = jnp.broadcast_to(key_mask[:, None, :], (user_count, events, key_mask.shape[1]))
    own_part = jnp.broadcast_to(causal[None, :, :], (user_count, events, events))
    weight_mask = jnp.concatenate([history_part, own_part], axis=2) * inv_count[:, None, None]
    query_heads = converter(own_query.reshape(user_count, events, HEADS, head_size))
    key_heads = converter(all_keys.reshape(user_count, -1, HEADS, head_size))
    value_heads = converter(all_values.reshape(user_count, -1, HEADS, head_size))
    scores = jnp.einsum(
        "bqhd,bkhd->bhqk", query_heads, key_heads, preferred_element_type=jnp.float32
    ) * (1.0 / math.sqrt(head_size))
    weights = (jax.nn.silu(scores) * weight_mask[:, None, :, :]).astype(jnp.bfloat16)
    mixed = jnp.einsum(
        "bhqk,bkhd->bqhd", converter(weights), value_heads, preferred_element_type=jnp.float32
    )
    return norm_rows(mixed.reshape(user_count * events, width)) * gate_units


def attend_groups(projected, history, key_mask, inv_count, groups):
    return attend(projected, history, key_mask, inv_count, keep_float)


def layer_forward(layer_input, w_in, w_out, attention):
    x_norm = norm_rows(layer_input.astype(jnp.float32)).astype(jnp.bfloat16)
    projected = jnp.dot(x_norm, w_in, preferred_element_type=jnp.float32)
    gated = attention(projected).astype(jnp.bfloat16)
    output_part = lax.dot_general(
        gated, w_out, (((1,), (1,)), ((), ())), preferred_element_type=jnp.float32
    )
    return (layer_input.astype(jnp.float32) + output_part).astype(jnp.bfloat16)


def layer_backward(layer_input, grad_y, w_in, w_out, attention):
    norm_value, norm_back = jax.vjp(norm_rows, layer_input.astype(jnp.float32))
    x_norm = norm_value.astype(jnp.bfloat16)
    projected = jnp.dot(x_norm, w_in, preferred_element_type=jnp.float32)
    gated_value, attend_back = jax.vjp(attention, projected)
    gated = gated_value.astype(jnp.bfloat16)
    grad_gated = jnp.dot(grad_y, w_out, preferred_element_type=jnp.float32)
    grad_projected = attend_back(grad_gated)[0].astype(jnp.bfloat16)
    grad_norm = lax.dot_general(
        grad_projected, w_in, (((1,), (1,)), ((), ())), preferred_element_type=jnp.float32
    )
    grad_x = (grad_y.astype(jnp.float32) + norm_back(grad_norm)[0]).astype(jnp.bfloat16)
    return (grad_x, x_norm, grad_projected, gated)


def contract_rows(left, right):
    return lax.dot_general(
        left, right, (((0,), (0,)), ((), ())), preferred_element_type=jnp.float32
    )


def store_rows(buffer, piece, is_valid):
    return jnp.where(is_valid, piece, buffer)


def body(
    embeddings,
    in_proj,
    out_proj,
    hist_cache,
    hist_len,
    block_mask,
    block_owner,
    block_slot,
    cotangent,
):
    sections = lax.axis_size("section")
    section_idx = lax.axis_index("section")
    owners = lax.axis_size("dp")
    user_count = hist_len.shape[0]
    requests = user_count * HBLK
    capacity = max(2, (5 * requests + 4 * owners - 1) // (4 * owners))
    w_in = in_proj[0]
    w_out = out_proj[0]
    cache_local = hist_cache[0]
    model_width = embeddings.shape[1]
    width = w_out.shape[1]
    owner_flat = block_owner.reshape(requests)
    slot_flat = block_slot.reshape(requests)
    request_order = jnp.arange(requests, dtype=jnp.int32)
    same_owner = (owner_flat[:, None] == owner_flat[None, :]) & (
        request_order[None, :] < request_order[:, None]
    )
    owner_rank = jnp.sum(same_owner.astype(jnp.int32), axis=1)
    target = owner_flat * capacity + owner_rank
    send_table = (
        jnp.zeros((owners * capacity,), jnp.int32)
        .at[target]
        .set(slot_flat)
        .reshape(owners, capacity)
    )
    outgoing = cache_local[
        lax.all_to_all(send_table, "dp", split_axis=0, concat_axis=0, tiled=True)
    ]
    fetched = lax.all_to_all(outgoing, "dp", split_axis=0, concat_axis=0, tiled=True)
    fetched = fetched.reshape(owners * capacity, EVT, 2 * width)
    events = event_mask(hist_len, block_mask)
    source = target.reshape(user_count, HBLK)
    live_flag = (jnp.max(events, axis=2) > 0).astype(jnp.int32)
    live_blocks = jnp.sum(live_flag, axis=1)
    history = fetched[source.reshape(requests)].reshape(user_count, HBLK * EVT, 2 * width)
    key_mask = events.reshape(user_count, HBLK * EVT)
    inv_count = 1.0 / (jnp.sum(key_mask, axis=1) + EVT)
    groups = (live_blocks + group_blocks - 1) // group_blocks
    micro_count = user_count // user_count
    micro_rows = user_count * EVT
    total_rows = user_count * EVT

    def attention_for():
        return partial(
            attend_groups,
            history=history,
            key_mask=key_mask,
            inv_count=inv_count,
            groups=jnp.max(groups),
        )

    def forward_step(step_index, loop_state):
        arriving, layer_out, layer_in = loop_state
        micro_index = step_index - section_idx
        is_valid = (micro_index >= 0) & (micro_index < micro_count)
        layer_input = jnp.where(section_idx == 0, embeddings, arriving)

        def run_layer(operand):
            return layer_forward(operand, w_in, w_out, attention_for())

        layer_result = lax.cond(is_valid, run_layer, jnp.zeros_like, layer_input)
        layer_in = store_rows(layer_in, layer_input, is_valid)
        layer_out = store_rows(layer_out, layer_result, is_valid)
        arriving = passed_along(layer_result, "section", 1)
        return (arriving, layer_out, layer_in)

    zeros_micro = jnp.zeros((micro_rows, model_width), jnp.bfloat16)
    zeros_total = jnp.zeros((total_rows, model_width), jnp.bfloat16)
    forward_state = lax.fori_loop(
        0, sections + micro_count - 1, forward_step, (zeros_micro, zeros_total, zeros_total)
    )
    layer_out = forward_state[1]
    layer_in = forward_state[2]

    def backward_step(step_index, loop_state):
        arriving, grad_out, kept_norm, kept_grad, kept_dy, kept_gated = loop_state
        micro_index = step_index - (sections - 1 - section_idx)
        is_valid = (micro_index >= 0) & (micro_index < micro_count)
        grad_y = jnp.where(section_idx == sections - 1, cotangent, arriving)

        def run_back(operands):
            return layer_backward(operands[0], operands[1], w_in, w_out, attention_for())

        def skip_back(operands):
            return (
                jnp.zeros((micro_rows, model_width), jnp.bfloat16),
                jnp.zeros((micro_rows, model_width), jnp.bfloat16),
                jnp.zeros((micro_rows, 4 * width), jnp.bfloat16),
                jnp.zeros((micro_rows, width), jnp.bfloat16),
            )

        grad_x, x_norm, grad_projected, gated = lax.cond(
            is_valid, run_back, skip_back, (layer_in, grad_y)
        )
        grad_out = store_rows(grad_out, grad_x, is_valid)
        kept_norm = store_rows(kept_norm, x_norm, is_valid)
        kept_grad = store_rows(kept_grad, grad_projected, is_valid)
        kept_dy = store_rows(kept_dy, grad_y, is_valid)
        kept_gated = store_rows(kept_gated, gated, is_valid)
        arriving = passed_along(grad_x, "section", -1)
        return (arriving, grad_out, kept_norm, kept_grad, kept_dy, kept_gated)

    backward_init = (
        zeros_micro,
        zeros_total,
        zeros_total,
        jnp.zeros((total_rows, 4 * width), jnp.bfloat16),
        zeros_total,
        jnp.zeros((total_rows, width), jnp.bfloat16),
    )
    backward_state = lax.fori_loop(0, sections + micro_count - 1, backward_step, backward_init)
    grad_out, kept_norm, kept_grad, kept_dy, kept_gated = backward_state[1:]
    own_rows = lax.psum_scatter(
        jnp.concatenate(
            [contract_rows(kept_norm, kept_grad), contract_rows(kept_dy, kept_gated)], axis=1
        ).astype(jnp.bfloat16),
        "dp",
        scatter_dimension=0,
        tiled=True,
    ).astype(jnp.float32)
    in_columns = 4 * width
    return (
        layer_out[None],
        grad_out[None],
        own_rows[None, :, :in_columns],
        own_rows[None, :, in_columns:],
    )


def solution(mesh):
    placed = (
        P("dp", None),
        P("section", None, None),
        P("section", None, None),
        P("section", "dp", None, None),
        P("dp"),
        P("dp", None),
        P("dp", None, None),
        P("dp", None),
        P("dp", None),
    )
    return jax.shard_map(
        body,
        mesh=mesh,
        in_specs=placed,
        out_specs=(
            P("section", "dp", None),
            P("section", "dp", None),
            P("section", "dp", None),
            P("section", "dp", None),
        ),
        check_vma=False,
    )
```

profile of v0, /device:TPU:0, one launch (start us, length us, event | category | flops | bytes accessed | tf_op | source)
XLA Modules:
  0.0 975.6 jit_solution(6537897233974777474)
XLA Ops:
  10.9 15.6 %all_to_all.17 = s32[32,1,2]{2,1,0:T(1,128)S(1)} all-to-all(s32[32,1,2]{2,1,0:T(1,128)S(1)} %bitcast.141), channel_id=1, replica_groups=mesh['section'=4,'dp'=32] {'dp'}, dimensions={0} | all-to-all | bytes 512 | tf_op jit(solution)/shard_map/all_to_all | solution.py:149
  26.8 9.8 %gather_fusion = bf16[64,128,1024]{2,1,0:T(8,128)(2,1)} fusion(bf16[16,128,1024]{2,1,0:T(8,128)(2,1)} %bitcast.128, s32[1024]{0:T(1024)S(1)} %pad_clamp_fusion.1), kind=kCustom, calls=%fused_computation | custom fusion | bytes 33554688 | tf_op jit(solution)/shard_map/gather | solution.py:148
  36.6 5.3 all-to-all-start.1
  42.8 240.1 %all-to-all-done.1 = bf16[32,2,128,1024]{3,2,1,0:T(8,128)(2,1)} async-done(((bf16[32,2,128,1024]{3,2,1,0:T(8,128)(2,1)}), bf16[32,2,128,1024]{3,2,1,0:T(8,128)(2,1)}, u32[]{:S(2)}, u32[]{:S(2)}) %all-to-all-start.1) | async-done | bytes 16777248 | tf_op jit(solution)/shard_map/all_to_all | solution.py:151
  282.9 10.9 %gather_fusion.1 = bf16[32,128,1024]{2,1,0:T(8,128)(2,1)} fusion(bf16[64,128,1024]{2,1,0:T(8,128)(2,1)} %bitcast.26, s32[1024]{0:T(1024)S(1)} %pad_clamp_fusion), kind=kCustom, calls=%fused_computation.1 | custom fusion | bytes 16777344 | tf_op jit(solution)/shard_map/gather | solution.py:157
  293.7 11.7 %copy.96 = bf16[2,2048,1024]{1,2,0:T(8,128)(2,1)} copy(bf16[2,2048,1024]{2,1,0:T(8,128)(2,1)} %bitcast.130) | data formatting | bytes 16777216
  305.5 149.9 %while.45 = (s32[]{:T(128)}, bf16[256,1024]{1,0:T(8,128)(2,1)S(1)}, bf16[256,1024]{1,0:T(8,128)(2,1)}, bf16[256,1024]{1,0:T(8,128)(2,1)S(1)}, s32[]{:T(128)}, /*...) while((s32[]{:T(128)}, bf16[256,1024]{1,0:T(8,128)(2,1)S(1)}, ...), condition=%wide.region_10.11_spmd.clone, body=%wide.region_3.10_spmd.clone.sunk | while | flops 2526130688 | bytes 69954928 | solution.py:191
  306.9 34.4 %conditional.6 = (bf16[256,1024]{1,0:T(8,128)(2,1)}) conditional(s32[]{:T(128)} %convert_element_type.237, () %tuple.131, (bf16[256,1024]{1,0:T(8,128)(2,1)S(1)}, bf16[2,2048,1024]{1,2,0:T(8,128)(2,1)}, bf16[1024,2048]{1,0:T(8,128)(2,1)}, f32[2,16,128]{2,1,0:T(8,128)S(1)}, f32[2]{0:T(128)}, /*index=5*/bf16[1024,512]{1,0:T(8,128)(2,1)}) %tuple.132), branch_computations={%region_4.4_spmd, %region_5.9_spmd} | conditional | flops 2524807680 | bytes 63638572 | solution.py:183
  306.9 6.1 fusion.80
  313.1 6.3 copy.77
  319.8 3.6 multiply_convert_fusion.1
  328.2 8.0 fusion.82
  338.6 2.6 fusion.11
  344.5 5.1 collective-permute-done
  351.8 36.7 %collective-permute-start = (bf16[256,1024]{1,0:T(8,128)(2,1)}, bf16[256,1024]{1,0:T(8,128)(2,1)S(1)}, u32[]{:S(2)}, u32[]{:S(2)}) collective-permute-start(bf16[256,1024]{1,0:T(8,128)(2,1)} %get-tuple-element.1289), channel_id=1, source_target_pairs={{0,32},{32,64},{64,96},{1,33},{33,65},{65,97},{2,34},{34,66},{66,9... | collective-permute-start | bytes 1572872 | tf_op jit(solution)/shard_map/while/body/eval_jaxpr/ppermute | solution.py:21
  390.5 9.6 collective-permute-done
  402.3 3.3 collective-permute-start
  407.5 5.1 collective-permute-done
  414.9 33.5 %collective-permute-start = (bf16[256,1024]{1,0:T(8,128)(2,1)}, bf16[256,1024]{1,0:T(8,128)(2,1)S(1)}, u32[]{:S(2)}, u32[]{:S(2)}) collective-permute-start(bf16[256,1024]{1,0:T(8,128)(2,1)} %get-tuple-element.1289), channel_id=1, source_target_pairs={{0,32},{32,64},{64,96},{1,33},{33,65},{65,97},{2,34},{34,66},{66,9... | collective-permute-start | bytes 1572872 | tf_op jit(solution)/shard_map/while/body/eval_jaxpr/ppermute | solution.py:21
  450.3 5.1 collective-permute-done
  456.2 375.1 %while.46 = (s32[]{:T(128)}, bf16[256,1024]{1,0:T(8,128)(2,1)}, bf16[256,1024]{1,0:T(8,128)(2,1)}, bf16[256,1024]{1,0:T(8,128)(2,1)}, bf16[256,2048]{1,0:T(8,128...) while((s32[]{:T(128)}, bf16[256,1024]{1,0:T(8,128)(2,1)}, ...), condition=%wide.region_22.23_spmd.clone, body=%wide.region_11.22_spmd.clone.sunk | while | flops 5948553728 | bytes 288567904 | solution.py:233
  458.3 3.5 conditional.7
  465.5 8.2 collective-permute-done.1
  473.9 2.1 select_select_fusion.15
  476.0 3.5 conditional.7
  482.7 2.3 select_select_fusion.16
  485.4 33.5 %collective-permute-done.1 = bf16[256,1024]{1,0:T(8,128)(2,1)} collective-permute-done((bf16[256,1024]{1,0:T(8,128)(2,1)}, bf16[256,1024]{1,0:T(8,128)(2,1)}, u32[]{:S(2)}, u32[]{:S(2)}) %collective-permute-start.1) | collective-permute-done | bytes 524320 | tf_op jit(solution)/shard_map/while/body/eval_jaxpr/ppermute | solution.py:21
  519.0 2.1 select_select_fusion.15
  521.2 3.5 conditional.7
  527.8 2.3 select_select_fusion.16
  530.5 213.9 %collective-permute-done.1 = bf16[256,1024]{1,0:T(8,128)(2,1)} collective-permute-done((bf16[256,1024]{1,0:T(8,128)(2,1)}, bf16[256,1024]{1,0:T(8,128)(2,1)}, u32[]{:S(2)}, u32[]{:S(2)}) %collective-permute-start.1) | collective-permute-done | bytes 524320 | tf_op jit(solution)/shard_map/while/body/eval_jaxpr/ppermute | solution.py:21
  744.6 2.1 select_select_fusion.15
  746.7 73.0 %conditional.7 = (bf16[256,1024]{1,0:T(8,128)(2,1)}, bf16[256,1024]{1,0:T(8,128)(2,1)}, bf16[256,2048]{1,0:T(8,128)(2,1)}, bf16[256,512]{1,0:T(8,128)(2,1)}) conditional(s32[]{:T(128)} %convert_element_type.239, () %tuple.136, (bf16[256,1024]{1,0:T(8,128)(2,1)S(1)}, bf16[1024,512]{1,0:T(8,128)(2,1)}, bf16[256,1024]{1,0:T(8,128)(2,1)S(1)}, ...), branch_computations={%region_12.12_spmd, %region_13.21_spmd} | conditional | flops 5945395712 | bytes 268291776 | solution.py:214
  749.4 4.1 multiply_convert_fusion.3
  762.0 6.2 fusion.87
  768.2 6.2 copy.82
  774.4 7.1 multiply_convert_fusion.2
  787.8 8.2 fusion.46
  796.1 2.0 fusion.59
  798.1 3.3 fusion.90
  801.4 3.7 convolution_convert_fusion
  812.6 2.9 fusion.51
  815.5 2.6 fusion.62
  822.9 2.6 select_select_fusion.16
  827.2 4.1 collective-permute-done.1
  832.9 2.7 convolution_convert_fusion.3
  835.5 2.7 pad_maximum_fusion.12
  838.3 128.2 %reduce-scatter.2.cloned.1.call-done = bf16[32,2560]{1,0:T(8,128)(2,1)} async-done(((bf16[1024,2560]{1,0:T(8,128)(2,1)}), bf16[32,2560]{1,0:T(8,128)(2,1)}) %reduce-scatter.2.cloned.1.call-update) | async-done | bytes 163856 | tf_op jit(solution)/shard_map/reduce_scatter | solution.py:235
  (252 shorter events, 91.8 us)
Async XLA Ops:
  36.6 5.5 copy-start.31
  36.6 5.5 copy-start.24
  36.6 246.3 %all-to-all-start.1 = ((bf16[32,2,128,1024]{3,2,1,0:T(8,128)(2,1)}), bf16[32,2,128,1024]{3,2,1,0:T(8,128)(2,1)}, u32[]{:S(2)}, u32[]{:S(2)}) async-start(bf16[32,2,128,1024]{3,2,1,0:T(8,128)(2,1)} %bitcast.127), calls=%async_computation.1 | async-start | bytes 33554432 | tf_op jit(solution)/shard_map/all_to_all | solution.py:151
  41.9 924.6 %reduce-scatter.2.cloned.1.call-start = ((), (), s32[]{:S(2)}) async-start(), calls=%async_computation.3 | async-start | bytes 5406720 | tf_op jit(solution)/shard_map/reduce_scatter | solution.py:235
  341.3 8.3 collective-permute-start
  351.8 48.2 %collective-permute-start = (bf16[256,1024]{1,0:T(8,128)(2,1)}, bf16[256,1024]{1,0:T(8,128)(2,1)S(1)}, u32[]{:S(2)}, u32[]{:S(2)}) collective-permute-start(bf16[256,1024]{1,0:T(8,128)(2,1)} %get-tuple-element.1289), channel_id=1, source_target_pairs={{0,32},{32,64},{64,96},{1,33},{33,65},{65,97},{2,34},{34,66},{66,9... | collective-permute-start | bytes 1572872 | tf_op jit(solution)/shard_map/while/body/eval_jaxpr/ppermute | solution.py:21
  402.3 10.2 %collective-permute-start = (bf16[256,1024]{1,0:T(8,128)(2,1)}, bf16[256,1024]{1,0:T(8,128)(2,1)S(1)}, u32[]{:S(2)}, u32[]{:S(2)}) collective-permute-start(bf16[256,1024]{1,0:T(8,128)(2,1)} %get-tuple-element.1289), channel_id=1, source_target_pairs={{0,32},{32,64},{64,96},{1,33},{33,65},{65,97},{2,34},{34,66},{66,9... | collective-permute-start | bytes 1572872 | tf_op jit(solution)/shard_map/while/body/eval_jaxpr/ppermute | solution.py:21
  414.9 40.5 %collective-permute-start = (bf16[256,1024]{1,0:T(8,128)(2,1)}, bf16[256,1024]{1,0:T(8,128)(2,1)S(1)}, u32[]{:S(2)}, u32[]{:S(2)}) collective-permute-start(bf16[256,1024]{1,0:T(8,128)(2,1)} %get-tuple-element.1289), channel_id=1, source_target_pairs={{0,32},{32,64},{64,96},{1,33},{33,65},{65,97},{2,34},{34,66},{66,9... | collective-permute-start | bytes 1572872 | tf_op jit(solution)/shard_map/while/body/eval_jaxpr/ppermute | solution.py:21
  461.8 3.3 copy-start.7
  461.8 11.9 %copy-start.17 = (s32[16,128]{1,0:T(8,128)S(1)}, s32[16,128]{1,0:T(8,128)}, u32[]{:S(2)}) copy-start(s32[16,128]{1,0:T(8,128)} %copy-done.16) | copy-start | bytes 24580 | tf_op jit(solution)/shard_map/while
  461.8 11.9 %copy-start.26 = (s32[2]{0:T(128)S(1)}, s32[2]{0:T(128)}, u32[]{:S(2)}) copy-start(s32[2]{0:T(128)} %copy-done.25) | copy-start | bytes 28 | tf_op jit(solution)/shard_map/while
  461.8 11.9 %copy-start.28 = (pred[2,16]{1,0:T(4,128)(4,1)S(1)}, pred[2,16]{1,0:T(4,128)(4,1)}, u32[]{:S(2)}) copy-start(pred[2,16]{1,0:T(4,128)(4,1)} %copy-done.27) | copy-start | bytes 100 | tf_op jit(solution)/shard_map/while
  461.8 11.9 %collective-permute-start.1 = (bf16[256,1024]{1,0:T(8,128)(2,1)}, bf16[256,1024]{1,0:T(8,128)(2,1)}, u32[]{:S(2)}, u32[]{:S(2)}) collective-permute-start(bf16[256,1024]{1,0:T(8,128)(2,1)} %get-tuple-element.1166), channel_id=1, source_target_pairs={{32,0},{64,32},{96,64},{33,1},{65,33},{97,65},{34,2},{66,34},{98,6... | collective-permute-start | bytes 1572872 | tf_op jit(solution)/shard_map/while/body/eval_jaxpr/ppermute | solution.py:21
  465.5 8.2 copy-start.8
  479.5 5.4 copy-start.7
  479.5 39.4 %copy-start.17 = (s32[16,128]{1,0:T(8,128)S(1)}, s32[16,128]{1,0:T(8,128)}, u32[]{:S(2)}) copy-start(s32[16,128]{1,0:T(8,128)} %copy-done.16) | copy-start | bytes 24580 | tf_op jit(solution)/shard_map/while
  479.5 39.4 %copy-start.26 = (s32[2]{0:T(128)S(1)}, s32[2]{0:T(128)}, u32[]{:S(2)}) copy-start(s32[2]{0:T(128)} %copy-done.25) | copy-start | bytes 28 | tf_op jit(solution)/shard_map/while
  479.5 39.4 %copy-start.28 = (pred[2,16]{1,0:T(4,128)(4,1)S(1)}, pred[2,16]{1,0:T(4,128)(4,1)}, u32[]{:S(2)}) copy-start(pred[2,16]{1,0:T(4,128)(4,1)} %copy-done.27) | copy-start | bytes 100 | tf_op jit(solution)/shard_map/while
  479.5 39.4 %collective-permute-start.1 = (bf16[256,1024]{1,0:T(8,128)(2,1)}, bf16[256,1024]{1,0:T(8,128)(2,1)}, u32[]{:S(2)}, u32[]{:S(2)}) collective-permute-start(bf16[256,1024]{1,0:T(8,128)(2,1)} %get-tuple-element.1166), channel_id=1, source_target_pairs={{32,0},{64,32},{96,64},{33,1},{65,33},{97,65},{34,2},{66,34},{98,6... | collective-permute-start | bytes 1572872 | tf_op jit(solution)/shard_map/while/body/eval_jaxpr/ppermute | solution.py:21
  485.3 33.5 %copy-start.8 = (bf16[256,2048]{1,0:T(8,128)(2,1)}, bf16[256,2048]{1,0:T(8,128)(2,1)S(1)}, u32[]{:S(2)}) copy-start(bf16[256,2048]{1,0:T(8,128)(2,1)S(1)} %select_select_fusion.17) | copy-start | bytes 3145732 | tf_op jit(solution)/shard_map/while
  524.7 5.4 copy-start.7
  524.7 219.7 %copy-start.17 = (s32[16,128]{1,0:T(8,128)S(1)}, s32[16,128]{1,0:T(8,128)}, u32[]{:S(2)}) copy-start(s32[16,128]{1,0:T(8,128)} %copy-done.16) | copy-start | bytes 24580 | tf_op jit(solution)/shard_map/while
  524.7 219.7 %copy-start.26 = (s32[2]{0:T(128)S(1)}, s32[2]{0:T(128)}, u32[]{:S(2)}) copy-start(s32[2]{0:T(128)} %copy-done.25) | copy-start | bytes 28 | tf_op jit(solution)/shard_map/while
  524.7 219.7 %copy-start.28 = (pred[2,16]{1,0:T(4,128)(4,1)S(1)}, pred[2,16]{1,0:T(4,128)(4,1)}, u32[]{:S(2)}) copy-start(pred[2,16]{1,0:T(4,128)(4,1)} %copy-done.27) | copy-start | bytes 100 | tf_op jit(solution)/shard_map/while
  524.7 219.7 %collective-permute-start.1 = (bf16[256,1024]{1,0:T(8,128)(2,1)}, bf16[256,1024]{1,0:T(8,128)(2,1)}, u32[]{:S(2)}, u32[]{:S(2)}) collective-permute-start(bf16[256,1024]{1,0:T(8,128)(2,1)} %get-tuple-element.1166), channel_id=1, source_target_pairs={{32,0},{64,32},{96,64},{33,1},{65,33},{97,65},{34,2},{66,34},{98,6... | collective-permute-start | bytes 1572872 | tf_op jit(solution)/shard_map/while/body/eval_jaxpr/ppermute | solution.py:21
  530.5 213.9 %copy-start.8 = (bf16[256,2048]{1,0:T(8,128)(2,1)}, bf16[256,2048]{1,0:T(8,128)(2,1)S(1)}, u32[]{:S(2)}) copy-start(bf16[256,2048]{1,0:T(8,128)(2,1)S(1)} %select_select_fusion.17) | copy-start | bytes 3145732 | tf_op jit(solution)/shard_map/while
  746.7 2.7 copy-start.29
  746.9 6.7 copy-start.18
  747.2 6.4 copy-start.22
  747.2 6.4 copy-start.20
  749.4 24.9 %copy-start.3 = (f32[2,128,2176]{2,1,0:T(8,128)}, f32[2,128,2176]{2,1,0:T(8,128)S(1)}, u32[]{:S(2)}) copy-start(f32[2,128,2176]{2,1,0:T(8,128)S(1)} %maximum_multiply_fusion.1) | copy-start | bytes 6684676 | tf_op jit(solution)/shard_map/while/body/eval_jaxpr/cond
  762.0 12.4 %copy-start.10 = (bf16[2,128,4,128]{1,3,2,0:T(8,128)(2,1)}, bf16[2,128,4,128]{1,3,2,0:T(8,128)(2,1)S(1)}, u32[]{:S(2)}) copy-start(bf16[2,128,4,128]{1,3,2,0:T(8,128)(2,1)S(1)} %copy.89) | copy-start | bytes 786436 | tf_op jit(solution)/shard_map/while/body/eval_jaxpr/cond
  774.4 7.1 copy-start.2
  774.4 7.1 copy-start.14
  787.8 8.3 copy-start.1
  787.8 8.3 copy-start.15
  798.1 3.3 copy-start.13
  801.4 11.1 %copy-start.4 = (f32[256,2048]{1,0:T(8,128)S(1)}, f32[256,2048]{1,0:T(8,128)}, u32[]{:S(2)}) copy-start(f32[256,2048]{1,0:T(8,128)} %get-tuple-element.948) | copy-start | bytes 6291460 | tf_op jit(solution)/shard_map/while/body/eval_jaxpr/cond
  805.2 10.3 %copy-start.19 = (f32[256]{0:T(256)S(1)}, f32[256]{0:T(256)}, u32[]{:S(2)}) copy-start(f32[256]{0:T(256)} %copy-done.18) | copy-start | bytes 3076 | tf_op jit(solution)/shard_map/while/body/eval_jaxpr/cond
  811.2 4.2 copy-start.30
  815.4 2.6 copy-start.23
  815.4 2.7 copy-start.21
  819.7 5.8 copy-start.7
  819.7 11.5 %copy-start.17 = (s32[16,128]{1,0:T(8,128)S(1)}, s32[16,128]{1,0:T(8,128)}, u32[]{:S(2)}) copy-start(s32[16,128]{1,0:T(8,128)} %copy-done.16) | copy-start | bytes 24580 | tf_op jit(solution)/shard_map/while
  819.7 11.5 %copy-start.26 = (s32[2]{0:T(128)S(1)}, s32[2]{0:T(128)}, u32[]{:S(2)}) copy-start(s32[2]{0:T(128)} %copy-done.25) | copy-start | bytes 28 | tf_op jit(solution)/shard_map/while
  819.7 11.5 %copy-start.28 = (pred[2,16]{1,0:T(4,128)(4,1)S(1)}, pred[2,16]{1,0:T(4,128)(4,1)}, u32[]{:S(2)}) copy-start(pred[2,16]{1,0:T(4,128)(4,1)} %copy-done.27) | copy-start | bytes 100 | tf_op jit(solution)/shard_map/while
  819.7 11.5 %collective-permute-start.1 = (bf16[256,1024]{1,0:T(8,128)(2,1)}, bf16[256,1024]{1,0:T(8,128)(2,1)}, u32[]{:S(2)}, u32[]{:S(2)}) collective-permute-start(bf16[256,1024]{1,0:T(8,128)(2,1)} %get-tuple-element.1166), channel_id=1, source_target_pairs={{32,0},{64,32},{96,64},{33,1},{65,33},{97,65},{34,2},{66,34},{98,6... | collective-permute-start | bytes 1572872 | tf_op jit(solution)/shard_map/while/body/eval_jaxpr/ppermute | solution.py:21
  827.2 4.1 copy-start.8
  (18 other events, 35.3 us)
Sparse Core Ops, SparseCore 0:
  838.4 128.0 reduce-scatter.1
where the time goes:
time: 978 us; the launch traced here: 976 us
  waiting for transfers between devices  653 us (67%)
  local copies, waits for them, and re-layouts  98.2 us (10%)
  starting transfers between devices  85.9 us (9%)
  other arithmetic  55.2 us (6%)
  matrix products  52.9 us (5%)
  blocking collectives  15.6 us (2%)
  between operations  14.2 us (1%)
    ppermute x8, waiting for transfers between devices, passed_along(): return lax.ppermute(array, axis, pairs)  284 us
    all_to_all x1, waiting for transfers between devices, body(): lax.all_to_all(outgoing, 'dp', split_axis=0, concat_axis=0, tiled=True)  240 us
    reduce_scatter x1, waiting for transfers between devices, body(): lax.psum_scatter(jnp.concatenate([contract_rows(kept_norm, kept_grad), co...  128 us
    ppermute x8, starting transfers between devices, passed_along(): return lax.ppermute(array, axis, pairs)  80.5 us
    select_n x24, other arithmetic, store_rows(): return jnp.where(is_valid, piece, buffer)  38.1 us
    dot_general x4, matrix products, attend(): jnp.einsum('bhqk,bkhd->bqhd', converter(weights), value_heads, preferred_...  21.4 us
  transfers between devices with their start and end apart: 10, of which 10 were waited for; matrix products, arithmetic and copies ran while one was open for 3% of the time, Pallas kernels for 0%

commit v1 on v0

v1 whole, which is shorter than its diff:
```python
from functools import partial
import math

import jax
import jax.numpy as jnp
from jax import lax
from jax.experimental import pallas as pl
from jax.experimental.pallas import tpu as pltpu
from jax.sharding import PartitionSpec as P

HEADS = 4
EVT = 128
HBLK = 16
USERS = 2
ROWS = USERS * EVT
D = 1024
HA = 512
HD = HA // HEADS
CAP = 2
GROUP = 4
KEYS = HBLK * EVT
OWNERS = 32
epsilon = 1e-06
SCALE = 1.0 / math.sqrt(HD)
MESH = pl.DeviceIdType.MESH
F32 = jnp.float32
BF16 = jnp.bfloat16


def dot(a, b, ca=1, cb=0):
    return lax.dot_general(a, b, (((ca,), (cb,)), ((), ())), preferred_element_type=F32)


def normed(values):
    centred = values - jnp.mean(values, axis=-1, keepdims=True)
    inverse = lax.rsqrt(jnp.mean(centred * centred, axis=-1, keepdims=True) + epsilon)
    return centred * inverse, inverse


def norm_back(grad, value, inverse):
    return inverse * (
        grad
        - jnp.mean(grad, axis=-1, keepdims=True)
        - value * jnp.mean(grad * value, axis=-1, keepdims=True)
    )


def silu_parts(half):
    t = jnp.tanh(half)
    return half + half * t, 0.5 * ((1.0 + t) + half * (1.0 - t * t))


def barrier_with(peers):
    barrier = pltpu.get_barrier_semaphore()
    for peer in peers:
        pl.semaphore_signal(barrier, inc=1, device_id=peer, device_id_type=MESH)
    pl.semaphore_wait(barrier, len(peers))


def exchange_kernel(
    table_ref, cache_ref, out_ref, asked, asked_s, outgoing, ask_send, ask_recv, send_sem, recv_sem, local_sem
):
    me = lax.axis_index("dp")
    barrier = pltpu.get_barrier_semaphore()

    def greet(i, carry):
        pl.semaphore_signal(
            barrier, inc=1, device_id={"dp": lax.rem(me + i, OWNERS)}, device_id_type=MESH
        )
        return carry

    lax.fori_loop(1, OWNERS, greet, 0)
    pl.semaphore_wait(barrier, OWNERS - 1)

    def ask(i):
        peer = lax.rem(me + i, OWNERS)
        return pltpu.make_async_remote_copy(
            src_ref=table_ref,
            dst_ref=asked.at[me],
            send_sem=ask_send.at[peer],
            recv_sem=ask_recv.at[me],
            device_id={"dp": peer},
            device_id_type=MESH,
        )

    def asked_by(i):
        peer = lax.rem(me + i, OWNERS)
        return pltpu.make_async_remote_copy(
            src_ref=table_ref,
            dst_ref=asked.at[peer],
            send_sem=ask_send.at[peer],
            recv_sem=ask_recv.at[peer],
            device_id={"dp": peer},
            device_id_type=MESH,
        )

    def start_ask(i, carry):
        ask(i).start()
        return carry

    lax.fori_loop(1, OWNERS, start_ask, 0)
    own = pltpu.make_async_copy(table_ref, asked.at[me], local_sem.at[0])
    own.start()
    own.wait()

    def wait_ask(i, carry):
        asked_by(i).wait()
        return carry

    lax.fori_loop(1, OWNERS, wait_ask, 0)
    down = pltpu.make_async_copy(asked, asked_s, local_sem.at[1])
    down.start()
    down.wait()

    def fill(peer):
        for k in range(CAP):
            outgoing[peer, k] = cache_ref[asked_s[peer, 0, me * CAP + k]]

    def send(i, carry):
        peer = lax.rem(me + i, OWNERS)
        fill(peer)
        pltpu.make_async_remote_copy(
            src_ref=outgoing.at[peer],
            dst_ref=out_ref.at[me],
            send_sem=send_sem.at[peer],
            recv_sem=recv_sem.at[me],
            device_id={"dp": peer},
            device_id_type=MESH,
        ).start()
        return carry

    lax.fori_loop(1, OWNERS, send, 0)
    fill(me)
    kept = pltpu.make_async_copy(outgoing.at[me], out_ref.at[me], local_sem.at[2])
    kept.start()

    def finish(i, carry):
        peer = lax.rem(me + i, OWNERS)
        pltpu.make_async_remote_copy(
            src_ref=outgoing.at[peer],
            dst_ref=out_ref.at[peer],
            send_sem=send_sem.at[peer],
            recv_sem=recv_sem.at[peer],
            device_id={"dp": peer},
            device_id_type=MESH,
        ).wait()
        return carry

    lax.fori_loop(1, OWNERS, finish, 0)
    kept.wait()


def exchange(table, cache):
    return pl.pallas_call(
        exchange_kernel,
        out_shape=jax.ShapeDtypeStruct((OWNERS, CAP, EVT, 2 * HA), BF16),
        in_specs=[pl.BlockSpec(memory_space=pltpu.VMEM)] * 2,
        out_specs=pl.BlockSpec(memory_space=pl.ANY),
        scratch_shapes=[
            pltpu.VMEM((OWNERS, 1, 128), jnp.int32),
            pltpu.SMEM((OWNERS, 1, 128), jnp.int32),
            pltpu.VMEM((OWNERS, CAP, EVT, 2 * HA), BF16),
            pltpu.SemaphoreType.DMA((OWNERS,)),
            pltpu.SemaphoreType.DMA((OWNERS,)),
            pltpu.SemaphoreType.DMA((OWNERS,)),
            pltpu.SemaphoreType.DMA((OWNERS,)),
            pltpu.SemaphoreType.DMA((3,)),
        ],
        compiler_params=pltpu.CompilerParams(
            collective_id=0, has_side_effects=True, vmem_limit_bytes=48 << 20
        ),
        name="exchange",
    )(table, cache)


def start_loads(where_ref, fetched_ref, hist, hist_sem):
    def one(r, carry):
        pltpu.make_async_copy(fetched_ref.at[where_ref[r]], hist.at[r], hist_sem.at[r]).start()
        return carry

    lax.fori_loop(0, USERS * HBLK, one, 0)


def wait_loads(fetched_ref, hist, hist_sem):
    def one(r, carry):
        pltpu.make_async_copy(fetched_ref.at[0], hist.at[r], hist_sem.at[r]).wait()
        return carry

    lax.fori_loop(0, USERS * HBLK, one, 0)


def mask_values(live_ref, hist):
    row = lax.broadcasted_iota(jnp.int32, (EVT, HA), 0)

    def one(r, carry):
        keep = (row < live_ref[r]).astype(F32).astype(BF16)
        hist[r, :, HA:] = hist[r, :, HA:] * keep
        return carry

    lax.fori_loop(0, USERS * HBLK, one, 0)


def inverse_count(live_ref, user):
    total = live_ref[user * HBLK]
    for j in range(1, HBLK):
        total = total + live_ref[user * HBLK + j]
    return 1.0 / (jnp.full((EVT, 1), total, jnp.int32).astype(F32) + float(EVT))


def columns(start):
    return pl.ds(pl.multiple_of(start, HD), HD)


def causal_mask():
    return lax.broadcasted_iota(jnp.int32, (EVT, EVT), 1) <= lax.broadcasted_iota(
        jnp.int32, (EVT, EVT), 0
    )


def attend_forward(act, hist, mixed, slope, own_weights, counts):
    causal = causal_mask()

    def one(index, carry):
        user, head = index // HEADS, index % HEADS
        rows = pl.ds(pl.multiple_of(user * EVT, EVT), EVT)
        query = act[rows, columns(2 * HA + head * HD)]
        total = jnp.zeros((EVT, HD), F32)
        for group in range(HBLK // GROUP):
            blocks = pl.ds(user * HBLK + group * GROUP, GROUP)
            keys = hist[blocks, :, columns(head * HD)].reshape(GROUP * EVT, HD)
            values = hist[blocks, :, columns(HA + head * HD)].reshape(GROUP * EVT, HD)
            weights, rise = silu_parts(dot(query, keys, 1, 1) * (0.5 * SCALE))
            total += dot(weights.astype(BF16), values)
            if slope is not None:
                slope[index, :, group * GROUP * EVT : (group + 1) * GROUP * EVT] = (
                    rise * SCALE
                ).astype(BF16)
        keys = act[rows, columns(3 * HA + head * HD)]
        values = act[rows, columns(HA + head * HD)]
        weights, rise = silu_parts(dot(query, keys, 1, 1) * (0.5 * SCALE))
        weights = jnp.where(causal, weights, 0.0).astype(BF16)
        total += dot(weights, values)
        if slope is not None:
            slope[index, :, KEYS:] = jnp.where(causal, rise * SCALE, 0.0).astype(BF16)
            own_weights[index] = weights
        mixed[rows, columns(head * HD)] = total * jnp.where(user == 0, counts[0], counts[1])
        return carry

    lax.fori_loop(0, USERS * HEADS, one, 0)


def forward_kernel(
    keep, where_ref, live_ref, x_ref, w_in_ref, w_out_ref, fetched_ref, *refs
):
    if keep:
        y_ref, x_norm_ref, act, slope_in, slope, own_weights, value_ref, gated_ref, rate_ref = refs[:9]
        refs = refs[9:]
    else:
        y_ref, refs = refs[0], refs[1:]
        slope = own_weights = None
        act, refs = refs[0], refs[1:]
    hist, mixed, hist_sem = refs
    start_loads(where_ref, fetched_ref, hist, hist_sem)
    x = x_ref[...].astype(F32)
    x_norm = normed(x)[0].astype(BF16)
    if keep:
        x_norm_ref[...] = x_norm
    for c in range(4):
        part = slice(c * HA, (c + 1) * HA)
        value, rise = silu_parts(dot(x_norm, w_in_ref[:, part]) * 0.5)
        act[:, part] = value.astype(BF16)
        if keep:
            slope_in[:, part] = rise
    wait_loads(fetched_ref, hist, hist_sem)
    mask_values(live_ref, hist)
    counts = [inverse_count(live_ref, user) for user in range(USERS)]
    attend_forward(act, hist, mixed, slope, own_weights, counts)
    value, rate = normed(mixed[...])
    gated = (value * act[:, :HA].astype(F32)).astype(BF16)
    if keep:
        value_ref[...] = value
        gated_ref[...] = gated
        rate_ref[...] = jnp.broadcast_to(rate, rate_ref.shape)
    y_ref[...] = (x + dot(gated, w_out_ref[...], 1, 1)).astype(BF16)


VM = pl.BlockSpec(memory_space=pltpu.VMEM)
SM = pl.BlockSpec(memory_space=pltpu.SMEM)
ANY = pl.BlockSpec(memory_space=pl.ANY)


def forward(where, live, x, w_in, w_out, fetched, keep):
    outs = [jax.ShapeDtypeStruct((ROWS, D), BF16)]
    scratch = [pltpu.VMEM((USERS * HBLK, EVT, 2 * HA), BF16), pltpu.VMEM((ROWS, HA), F32)]
    scratch += [pltpu.SemaphoreType.DMA((USERS * HBLK,))]
    if keep:
        outs += [
            jax.ShapeDtypeStruct((ROWS, D), BF16),
            jax.ShapeDtypeStruct((ROWS, 4 * HA), BF16),
            jax.ShapeDtypeStruct((ROWS, 4 * HA), F32),
            jax.ShapeDtypeStruct((USERS * HEADS, EVT, KEYS + EVT), BF16),
            jax.ShapeDtypeStruct((USERS * HEADS, EVT, EVT), BF16),
            jax.ShapeDtypeStruct((ROWS, HA), F32),
            jax.ShapeDtypeStruct((ROWS, HA), BF16),
            jax.ShapeDtypeStruct((ROWS, 128), F32),
        ]
    else:
        scratch = [pltpu.VMEM((ROWS, 4 * HA), BF16)] + scratch
    return pl.pallas_call(
        partial(forward_kernel, keep),
        out_shape=outs,
        in_specs=[SM, SM, VM, VM, VM, ANY],
        out_specs=[VM] * len(outs),
        scratch_shapes=scratch,
        compiler_params=pltpu.CompilerParams(vmem_limit_bytes=52 << 20),
        name="forward_keep" if keep else "forward",
    )(where, live, x, w_in, w_out, fetched)


def backward_kernel(
    where_ref, live_ref, x_ref, dy_ref, w_in_ref, w_out_ref, fetched_ref,
    act, slope_in, slope, own_weights, value_ref, rate_ref,
    dx_ref, dproj, hist, dmixed, hist_sem,
):
    start_loads(where_ref, fetched_ref, hist, hist_sem)
    dy = dy_ref[...]
    dgated = dot(dy, w_out_ref[...])
    value = value_ref[...]
    dproj[:, :HA] = (dgated * value * slope_in[:, :HA]).astype(BF16)
    grad = norm_back(dgated * act[:, :HA].astype(F32), value, rate_ref[:, :1])
    for user in range(USERS):
        rows = slice(user * EVT, (user + 1) * EVT)
        dmixed[rows] = (grad[rows] * inverse_count(live_ref, user)).astype(BF16)
    wait_loads(fetched_ref, hist, hist_sem)
    mask_values(live_ref, hist)

    def one(index, carry):
        user, head = index // HEADS, index % HEADS
        rows = pl.ds(pl.multiple_of(user * EVT, EVT), EVT)
        grad_mixed = dmixed[rows, columns(head * HD)]
        total = jnp.zeros((EVT, HD), F32)
        for group in range(HBLK // GROUP):
            blocks = pl.ds(user * HBLK + group * GROUP, GROUP)
            keys = hist[blocks, :, columns(head * HD)].reshape(GROUP * EVT, HD)
            values = hist[blocks, :, columns(HA + head * HD)].reshape(GROUP * EVT, HD)
            rise = slope[index, :, group * GROUP * EVT : (group + 1) * GROUP * EVT].astype(F32)
            ds = (dot(grad_mixed, values, 1, 1) * rise).astype(BF16)
            total += dot(ds, keys)
        query = act[rows, columns(2 * HA + head * HD)]
        keys = act[rows, columns(3 * HA + head * HD)]
        values = act[rows, columns(HA + head * HD)]
        ds = (dot(grad_mixed, values, 1, 1) * slope[index, :, KEYS:].astype(F32)).astype(BF16)
        total += dot(ds, keys)
        dvalue = dot(own_weights[index], grad_mixed, 0, 0)
        dkey = dot(ds, query, 0, 0)
        for base, part in ((HA, dvalue), (2 * HA, total), (3 * HA, dkey)):
            at = columns(base + head * HD)
            dproj[rows, at] = (part * slope_in[rows, at]).astype(BF16)
        return carry

    lax.fori_loop(0, USERS * HEADS, one, 0)
    dnorm = dot(dproj[...], w_in_ref[...], 1, 1)
    x_norm, rate = normed(x_ref[...].astype(F32))
    dx_ref[...] = (dy.astype(F32) + norm_back(dnorm, x_norm, rate)).astype(BF16)


def backward(where, live, x, dy, w_in, w_out, fetched, kept):
    return pl.pallas_call(
        backward_kernel,
        out_shape=[
            jax.ShapeDtypeStruct((ROWS, D), BF16),
            jax.ShapeDtypeStruct((ROWS, 4 * HA), BF16),
        ],
        in_specs=[SM, SM, VM, VM, VM, VM, ANY] + [VM] * 6,
        out_specs=[VM, VM],
        scratch_shapes=[
            pltpu.VMEM((USERS * HBLK, EVT, 2 * HA), BF16),
            pltpu.VMEM((ROWS, HA), BF16),
            pltpu.SemaphoreType.DMA((USERS * HBLK,)),
        ],
        compiler_params=pltpu.CompilerParams(vmem_limit_bytes=52 << 20),
        name="backward",
    )(where, live, x, dy, w_in, w_out, fetched, *kept)


def passed_along(array, axis, by):
    peers = lax.axis_size(axis)
    pairs = [(i, i + by) for i in range(peers) if 0 <= i + by < peers]
    return lax.ppermute(array, axis, pairs)


def body(
    embeddings, in_proj, out_proj, hist_cache, hist_len, block_mask, block_owner, block_slot, cotangent
):
    sections = lax.axis_size("section")
    section = lax.axis_index("section")
    w_in, w_out = in_proj[0], out_proj[0]
    requests = USERS * HBLK
    owner = block_owner.reshape(requests)
    order = jnp.arange(requests, dtype=jnp.int32)
    earlier = (owner[:, None] == owner[None, :]) & (order[None, :] < order[:, None])
    where = owner * CAP + jnp.sum(earlier.astype(jnp.int32), axis=1)
    names = jnp.arange(128, dtype=jnp.int32)
    table = jnp.sum(
        jnp.where(where[:, None] == names[None, :], block_slot.reshape(requests, 1), 0), axis=0
    )
    start = jnp.arange(HBLK, dtype=jnp.int32)[None, :] * EVT
    live = jnp.where(block_mask > 0, jnp.clip(hist_len[:, None] - start, 0, EVT), 0).reshape(requests)
    fetched = exchange(table.reshape(1, 128), hist_cache[0]).reshape(OWNERS * CAP, EVT, 2 * HA)

    x = embeddings
    for step in range(sections):
        made = forward(where, live, x, w_in, w_out, fetched, step == sections - 1)
        if step < sections - 1:
            arriving = passed_along(made[0], "section", 1)
            x = jnp.where(section == step + 1, arriving, x)
    y, x_norm, act, slope_in, slope, own_weights, value, gated, rate = made
    dy = cotangent
    kept = (act, slope_in, slope, own_weights, value, rate)
    for step in reversed(range(sections)):
        dx, dproj = backward(where, live, x, dy, w_in, w_out, fetched, kept)
        if step > 0:
            arriving = passed_along(dx, "section", -1)
            dy = jnp.where(section == step - 1, arriving, dy)
    own_rows = lax.psum_scatter(
        jnp.concatenate([dot(x_norm, dproj, 0, 0), dot(dy, gated, 0, 0)], axis=1).astype(BF16),
        "dp",
        scatter_dimension=0,
        tiled=True,
    ).astype(F32)
    return (y[None], dx[None], own_rows[None, :, : 4 * HA], own_rows[None, :, 4 * HA :])


def solution(mesh):
    placed = (
        P("dp", None),
        P("section", None, None),
        P("section", None, None),
        P("section", "dp", None, None),
        P("dp"),
        P("dp", None),
        P("dp", None, None),
        P("dp", None),
        P("dp", None),
    )
    return jax.shard_map(
        body,
        mesh=mesh,
        in_specs=placed,
        out_specs=(
            P("section", "dp", None),
            P("section", "dp", None),
            P("section", "dp", None),
            P("section", "dp", None),
        ),
        check_vma=False,
    )
```

time: 978 us -> 722 us (0.74)
  Pallas kernels: 0 us -> 477 us
  waiting for transfers between devices: 653 us -> 197 us
  local copies, waits for them, and re-layouts: 98.2 us -> 5.87 us
  starting transfers between devices: 85.9 us -> 16.6 us
  matrix products: 52.9 us -> 3 us
  other arithmetic: 55.2 us -> 8.23 us
  blocking collectives: 15.6 us -> 0 us
    pallas_call x0 -> x9, Pallas kernels: none -> 477 us  [the longest x1 336 us: exchange(): pl.pallas_call(exchange_kernel, out_shape=jax.ShapeDtypeStruct((OWNERS, C...]
    all_to_all x1 -> x0, waiting for transfers between devices: 240 us -> none  [body(): lax.all_to_all(outgoing, 'dp', split_axis=0, concat_axis=0, tiled=True)]
    ppermute x8 -> x6, waiting for transfers between devices: 284 us -> 60 us  [passed_along(): return lax.ppermute(array, axis, pairs)]
    ppermute x8 -> x6, starting transfers between devices: 80.5 us -> 16.5 us  [passed_along(): return lax.ppermute(array, axis, pairs)]
    dot_general x14 -> x2, matrix products: 52.9 us -> 3 us  [dot(): lax.dot_general(a, b, (((ca,), (cb,)), ((), ())), preferred_element_type=...]
    select_n x26 -> x7, other arithmetic: 38.2 us -> 2.95 us  [the longest x3 1.24 us: body(): dy = jnp.where(section == step - 1, arriving, dy)]
    gather x2 -> x0, local copies, waits for them, and re-layouts: 20.6 us -> none  [the longest x1 10.9 us: body(): fetched[source.reshape(requests)].reshape(user_count, HBLK * EVT, 2 * width)]
    concatenate x10 -> x0, local copies, waits for them, and re-layouts: 17.9 us -> none  [the longest x6 15 us: attend(): jnp.concatenate([history[:, :, :width], own_key.reshape(user_count, event...]
  transfers between devices with their start and end apart: 10 -> 7, of which waited for: 10 -> 7; matrix products, arithmetic and copies ran while one was open for 3% -> 0% of each run, Pallas kernels for 0% -> 0%
where the time goes in v1:
time: 722 us
  Pallas kernels  477 us (66%)
  waiting for transfers between devices  197 us (27%)
  starting transfers between devices  16.6 us (2%)
  between operations  14.2 us (2%)
  other arithmetic  8.23 us (1%)
    pallas_call x1, Pallas kernels, exchange(): pl.pallas_call(exchange_kernel, out_shape=jax.ShapeDtypeStruct((OWNERS, C...  336 us
    reduce_scatter x1, waiting for transfers between devices, body(): lax.psum_scatter(jnp.concatenate([dot(x_norm, dproj, 0, 0), dot(dy, gated...  137 us
    pallas_call x4, Pallas kernels, backward(): pl.pallas_call(backward_kernel, out_shape=[jax.ShapeDtypeStruct((ROWS, D)...  74.8 us
    pallas_call x4, Pallas kernels, forward(): pl.pallas_call(partial(forward_kernel, keep), out_shape=outs, in_specs=[S...  66.4 us
    ppermute x6, waiting for transfers between devices, passed_along(): return lax.ppermute(array, axis, pairs)  60 us
    ppermute x6, starting transfers between devices, passed_along(): return lax.ppermute(array, axis, pairs)  16.5 us
  transfers between devices with their start and end apart: 7, of which 7 were waited for; matrix products, arithmetic and copies ran while one was open for 0% of the time, Pallas kernels for 0%

profile of v1, /device:TPU:0, one launch (start us, length us, event | category | flops | bytes accessed | tf_op | source)
XLA Modules:
  0.0 721.6 jit_solution(16476180718005201246)
XLA Ops:
  7.2 0.0 reduce-scatter.2.cloned.1.call-start
  7.2 0.5 broadcast.18
  7.7 1.3 reduce.3
  9.1 0.1 reshape.38
  9.2 0.2 convert_reduce_fusion
  9.3 0.8 broadcast_in_dim.34
  10.1 0.8 compare_select_fusion
  10.9 0.1 reshape.39.live_ref
  10.9 0.1 select_reduce_fusion
  11.0 2.2 copy-done.3
  13.2 335.9 %exchange.1 = bf16[32,2,128,1024]{3,2,1,0:T(8,128)(2,1)} custom-call(s32[1,128]{1,0:T(1,128)S(1)} %bitcast.17, bf16[16,128,1024]{2,1,0:T(8,128)(2,1)S(1)} %bitcast.16), custom_call_target="tpu_custom_call" | custom-call | tf_op jit(solution)/shard_map/exchange/pallas_call | solution.py:154
  349.2 15.4 %forward.3 = bf16[256,1024]{1,0:T(8,128)(2,1)S(1)} custom-call(s32[32]{0:T(128)S(1)} %multiply_add_fusion.where_ref, s32[32]{0:T(128)S(1)} %reshape.39.live_ref, bf16[256,1024]{1,0:T(8,128)(2,1)S(1)} %copy-done.5, bf16[1024,2048]{1,0:T(8,128)(2,1)} %bitcast.26, bf16[1024,512]{1,0:T(8,128)(2,1)} %bitcast.34, bf16[64,128,1024]{2,1,0:T(8,128)(2,1)} %bitcast.18), custom_call_target="tpu_custom_call" | custom-call | tf_op jit(solution)/shard_map/forward/pallas_call | solution.py:309
  364.6 3.4 collective-permute-start
  368.0 10.5 %collective-permute-done = bf16[256,1024]{1,0:T(8,128)(2,1)S(1)} collective-permute-done((bf16[256,1024]{1,0:T(8,128)(2,1)S(1)}, bf16[256,1024]{1,0:T(8,128)(2,1)S(1)}, u32[]{:S(2)}, u32[]{:S(2)}) %collective-permute-start) | collective-permute-done | bytes 524320 | tf_op jit(solution)/shard_map/ppermute | solution.py:389
  378.5 0.1 broadcast_select_fusion.2.x_ref
  378.6 15.4 %forward.4 = bf16[256,1024]{1,0:T(8,128)(2,1)S(1)} custom-call(s32[32]{0:T(128)S(1)} %multiply_add_fusion.where_ref, s32[32]{0:T(128)S(1)} %reshape.39.live_ref, bf16[256,1024]{1,0:T(8,128)(2,1)S(1)} %broadcast_select_fusion.2.x_ref, bf16[1024,2048]{1,0:T(8,128)(2,1)} %bitcast.27, bf16[1024,512]{1,0:T(8,128)(2,1)} %bitcast.35, bf16[64,128,1024]{2,1,0:T(8,128)(2,1)} %bitcast.19), custom_call_target="tpu_custom_call" | custom-call | tf_op jit(solution)/shard_map/forward/pallas_call | solution.py:309
  394.0 4.4 collective-permute-start.1
  398.4 9.6 %collective-permute-done.1 = bf16[256,1024]{1,0:T(8,128)(2,1)S(1)} collective-permute-done((bf16[256,1024]{1,0:T(8,128)(2,1)S(1)}, bf16[256,1024]{1,0:T(8,128)(2,1)S(1)}, u32[]{:S(2)}, u32[]{:S(2)}) %collective-permute-start.1) | collective-permute-done | bytes 524320 | tf_op jit(solution)/shard_map/ppermute | solution.py:389
  408.0 0.1 broadcast_select_fusion.4.x_ref
  408.1 15.4 %forward.5 = bf16[256,1024]{1,0:T(8,128)(2,1)S(1)} custom-call(s32[32]{0:T(128)S(1)} %multiply_add_fusion.where_ref, s32[32]{0:T(128)S(1)} %reshape.39.live_ref, bf16[256,1024]{1,0:T(8,128)(2,1)S(1)} %broadcast_select_fusion.4.x_ref, bf16[1024,2048]{1,0:T(8,128)(2,1)} %bitcast.28, bf16[1024,512]{1,0:T(8,128)(2,1)} %bitcast.36, bf16[64,128,1024]{2,1,0:T(8,128)(2,1)} %bitcast.20), custom_call_target="tpu_custom_call" | custom-call | tf_op jit(solution)/shard_map/forward/pallas_call | solution.py:309
  423.5 4.6 collective-permute-start.2
  428.1 8.5 %collective-permute-done.2 = bf16[256,1024]{1,0:T(8,128)(2,1)S(1)} collective-permute-done((bf16[256,1024]{1,0:T(8,128)(2,1)S(1)}, bf16[256,1024]{1,0:T(8,128)(2,1)S(1)}, u32[]{:S(2)}, u32[]{:S(2)}) %collective-permute-start.2) | collective-permute-done | bytes 524320 | tf_op jit(solution)/shard_map/ppermute | solution.py:389
  436.6 0.8 broadcast_select_fusion.5.x_ref
  437.4 20.2 %forward_keep.1 = (bf16[256,1024]{1,0:T(8,128)(2,1)}, bf16[256,1024]{1,0:T(8,128)(2,1)S(1)}, bf16[256,2048]{1,0:T(8,128)(2,1)}, f32[256,2048]{1,0:T(8,128)}, bf1...) custom-call(s32[32]{0:T(128)S(1)} %multiply_add_fusion.where_ref, ...), custom_call_target="tpu_custom_call" | custom-call | tf_op jit(solution)/shard_map/forward_keep/pallas_call | solution.py:309
  457.6 0.0 copy-start.1
  457.6 0.9 copy-done.1
  458.5 18.5 %backward.4 = (bf16[256,1024]{1,0:T(8,128)(2,1)S(1)}, bf16[256,2048]{1,0:T(8,128)(2,1)}) custom-call(s32[32]{0:T(128)S(1)} %multiply_add_fusion.where_ref, s32[32]{0:T(128)S(1)} %reshape.39.live_ref, bf16[256,1024]{1,0:T(8,128)(2,1)S(1)} %copy-done, bf16[256,1024]{1,0:T(8,128)(2,1)S(1)} %copy-done.4, bf16[1024,2048]{1,0:T(8,128)(2,1)} %bitcast.30, ...), custom_call_target="tpu_custom_call" | custom-call | tf_op jit(solution)/shard_map/backward/pallas_call | solution.py:368
  477.0 1.3 collective-permute-start.3
  478.3 11.6 %collective-permute-done.3 = bf16[256,1024]{1,0:T(8,128)(2,1)S(1)} collective-permute-done((bf16[256,1024]{1,0:T(8,128)(2,1)S(1)}, bf16[256,1024]{1,0:T(8,128)(2,1)S(1)}, u32[]{:S(2)}, u32[]{:S(2)}) %collective-permute-start.3) | collective-permute-done | bytes 524320 | tf_op jit(solution)/shard_map/ppermute | solution.py:389
  489.9 0.1 broadcast_select_fusion.3.dy_ref
  489.9 18.5 %backward.5 = (bf16[256,1024]{1,0:T(8,128)(2,1)S(1)}, bf16[256,2048]{1,0:T(8,128)(2,1)}) custom-call(s32[32]{0:T(128)S(1)} %multiply_add_fusion.where_ref, s32[32]{0:T(128)S(1)} %reshape.39.live_ref, bf16[256,1024]{1,0:T(8,128)(2,1)S(1)} %copy-done, bf16[256,1024]{1,0:T(8,128)(2,1)S(1)} %broadcast_select_fusion.3.dy_ref, bf16[1024,2048]{1,0:T(8,128)(2,1)} %bitcast.31, ...), custom_call_target="tpu_custom_call" | custom-call | tf_op jit(solution)/shard_map/backward/pallas_call | solution.py:368
  508.4 1.3 collective-permute-start.4
  509.7 10.2 %collective-permute-done.4 = bf16[256,1024]{1,0:T(8,128)(2,1)S(1)} collective-permute-done((bf16[256,1024]{1,0:T(8,128)(2,1)S(1)}, bf16[256,1024]{1,0:T(8,128)(2,1)S(1)}, u32[]{:S(2)}, u32[]{:S(2)}) %collective-permute-start.4) | collective-permute-done | bytes 524320 | tf_op jit(solution)/shard_map/ppermute | solution.py:389
  519.9 0.1 broadcast_select_fusion.1.dy_ref
  520.0 18.5 %backward.6 = (bf16[256,1024]{1,0:T(8,128)(2,1)S(1)}, bf16[256,2048]{1,0:T(8,128)(2,1)}) custom-call(s32[32]{0:T(128)S(1)} %multiply_add_fusion.where_ref, s32[32]{0:T(128)S(1)} %reshape.39.live_ref, bf16[256,1024]{1,0:T(8,128)(2,1)S(1)} %copy-done, bf16[256,1024]{1,0:T(8,128)(2,1)S(1)} %broadcast_select_fusion.1.dy_ref, bf16[1024,2048]{1,0:T(8,128)(2,1)} %bitcast.32, ...), custom_call_target="tpu_custom_call" | custom-call | tf_op jit(solution)/shard_map/backward/pallas_call | solution.py:368
  538.5 1.5 collective-permute-start.5
  540.1 9.7 %collective-permute-done.5 = bf16[256,1024]{1,0:T(8,128)(2,1)} collective-permute-done((bf16[256,1024]{1,0:T(8,128)(2,1)S(1)}, bf16[256,1024]{1,0:T(8,128)(2,1)}, u32[]{:S(2)}, u32[]{:S(2)}) %collective-permute-start.5) | collective-permute-done | bytes 524320 | tf_op jit(solution)/shard_map/ppermute | solution.py:389
  549.7 1.1 broadcast_select_fusion.dy_ref
  550.8 0.0 copy-done.2
  550.9 19.3 %backward.7 = (bf16[256,1024]{1,0:T(8,128)(2,1)}, bf16[256,2048]{1,0:T(8,128)(2,1)}) custom-call(s32[32]{0:T(128)S(1)} %multiply_add_fusion.where_ref, s32[32]{0:T(128)S(1)} %reshape.39.live_ref, bf16[256,1024]{1,0:T(8,128)(2,1)S(1)} %copy-done, bf16[256,1024]{1,0:T(8,128)(2,1)S(1)} %broadcast_select_fusion.dy_ref, bf16[1024,2048]{1,0:T(8,128)(2,1)} %bitcast.33, ...), custom_call_target="tpu_custom_call" | custom-call | tf_op jit(solution)/shard_map/backward/pallas_call | solution.py:368
  570.1 0.5 convolution_convert_fusion.1
  570.6 2.5 convolution_convert_fusion
  573.1 2.7 pad_maximum_fusion
  575.9 0.0 reduce-scatter.2.cloned.1.call-update
  575.9 136.6 %reduce-scatter.2.cloned.1.call-done = bf16[32,2560]{1,0:T(8,128)(2,1)} async-done(((bf16[1024,2560]{1,0:T(8,128)(2,1)}), bf16[32,2560]{1,0:T(8,128)(2,1)}) %reduce-scatter.2.cloned.1.call-update) | async-done | bytes 163856 | tf_op jit(solution)/shard_map/reduce_scatter | solution.py:425
  712.4 0.9 convert_element_type.8
  713.4 0.6 slice_bitcast_fusion.1
  714.0 0.7 slice_bitcast_fusion
  (10 shorter events, 0.0 us)
Async XLA Ops:
  7.2 705.3 %reduce-scatter.2.cloned.1.call-start = ((), (), s32[]{:S(2)}) async-start(), calls=%async_computation.1 | async-start | bytes 5406720 | tf_op jit(solution)/shard_map/reduce_scatter | solution.py:425
  11.0 2.2 copy-start.3
  13.2 335.9 %copy-start.5 = (bf16[256,1024]{1,0:T(8,128)(2,1)S(1)}, bf16[256,1024]{1,0:T(8,128)(2,1)}, u32[]{:S(2)}) copy-start(bf16[256,1024]{1,0:T(8,128)(2,1)} %x_ref.1) | copy-start | bytes 1572868
  364.6 13.9 %collective-permute-start = (bf16[256,1024]{1,0:T(8,128)(2,1)S(1)}, bf16[256,1024]{1,0:T(8,128)(2,1)S(1)}, u32[]{:S(2)}, u32[]{:S(2)}) collective-permute-start(bf16[256,1024]{1,0:T(8,128)(2,1)S(1)} %forward.3), channel_id=1, source_target_pairs={{0,32},{32,64},{64,96},{1,33},{33,65},{65,97},{2,34},{34,66},{66,9... | collective-permute-start | bytes 1572872 | tf_op jit(solution)/shard_map/ppermute | solution.py:389
  394.0 14.0 %collective-permute-start.1 = (bf16[256,1024]{1,0:T(8,128)(2,1)S(1)}, bf16[256,1024]{1,0:T(8,128)(2,1)S(1)}, u32[]{:S(2)}, u32[]{:S(2)}) collective-permute-start(bf16[256,1024]{1,0:T(8,128)(2,1)S(1)} %forward.4), channel_id=1, source_target_pairs={{0,32},{32,64},{64,96},{1,33},{33,65},{65,97},{2,34},{34,66},{66,9... | collective-permute-start | bytes 1572872 | tf_op jit(solution)/shard_map/ppermute | solution.py:389
  423.5 13.1 %collective-permute-start.2 = (bf16[256,1024]{1,0:T(8,128)(2,1)S(1)}, bf16[256,1024]{1,0:T(8,128)(2,1)S(1)}, u32[]{:S(2)}, u32[]{:S(2)}) collective-permute-start(bf16[256,1024]{1,0:T(8,128)(2,1)S(1)} %forward.5), channel_id=1, source_target_pairs={{0,32},{32,64},{64,96},{1,33},{33,65},{65,97},{2,34},{34,66},{66,9... | collective-permute-start | bytes 1572872 | tf_op jit(solution)/shard_map/ppermute | solution.py:389
  437.4 21.1 %copy-start = (bf16[256,1024]{1,0:T(8,128)(2,1)S(1)}, bf16[256,1024]{1,0:T(8,128)(2,1)}, u32[]{:S(2)}) copy-start(bf16[256,1024]{1,0:T(8,128)(2,1)} %broadcast_select_fusion.5.x_ref) | copy-start | bytes 1572868
  437.4 21.1 %copy-start.4 = (bf16[256,1024]{1,0:T(8,128)(2,1)S(1)}, bf16[256,1024]{1,0:T(8,128)(2,1)}, u32[]{:S(2)}) copy-start(bf16[256,1024]{1,0:T(8,128)(2,1)} %dy_ref.1) | copy-start | bytes 1572868
  457.6 0.9 copy-start.1
  477.0 12.9 %collective-permute-start.3 = (bf16[256,1024]{1,0:T(8,128)(2,1)S(1)}, bf16[256,1024]{1,0:T(8,128)(2,1)S(1)}, u32[]{:S(2)}, u32[]{:S(2)}) collective-permute-start(bf16[256,1024]{1,0:T(8,128)(2,1)S(1)} %get-tuple-element.25), channel_id=1, source_target_pairs={{32,0},{64,32},{96,64},{33,1},{65,33},{97,65},{34,2},{66,34},{98,6... | collective-permute-start | bytes 1572872 | tf_op jit(solution)/shard_map/ppermute | solution.py:389
  508.4 11.5 %collective-permute-start.4 = (bf16[256,1024]{1,0:T(8,128)(2,1)S(1)}, bf16[256,1024]{1,0:T(8,128)(2,1)S(1)}, u32[]{:S(2)}, u32[]{:S(2)}) collective-permute-start(bf16[256,1024]{1,0:T(8,128)(2,1)S(1)} %get-tuple-element.26), channel_id=1, source_target_pairs={{32,0},{64,32},{96,64},{33,1},{65,33},{97,65},{34,2},{66,34},{98,6... | collective-permute-start | bytes 1572872 | tf_op jit(solution)/shard_map/ppermute | solution.py:389
  520.0 30.9 %copy-start.2 = (f32[256,512]{1,0:T(8,128)S(1)}, f32[256,512]{1,0:T(8,128)}, u32[]{:S(2)}) copy-start(f32[256,512]{1,0:T(8,128)} %copy-done.1) | copy-start | bytes 1572868
  538.5 11.2 %collective-permute-start.5 = (bf16[256,1024]{1,0:T(8,128)(2,1)S(1)}, bf16[256,1024]{1,0:T(8,128)(2,1)}, u32[]{:S(2)}, u32[]{:S(2)}) collective-permute-start(bf16[256,1024]{1,0:T(8,128)(2,1)S(1)} %get-tuple-element.27), channel_id=1, source_target_pairs={{32,0},{64,32},{96,64},{33,1},{65,33},{97,65},{34,2},{66,34},{98,6... | collective-permute-start | bytes 1572872 | tf_op jit(solution)/shard_map/ppermute | solution.py:389
Sparse Core Ops, SparseCore 0:
  576.0 136.3 reduce-scatter.1

commit v2 on v1

--- a/solution.py
+++ b/solution.py
@@ -57,96 +57,77 @@
     pl.semaphore_wait(barrier, len(peers))
 
 
+def chip_at(offset):
+    me = lax.axis_index("dp")
+    y, z, c = me // 8, lax.rem(me // 2, 4), lax.rem(me, 2)
+    return (
+        lax.rem(y + offset[0] + 4, 4) * 8 + lax.rem(z + offset[1] + 4, 4) * 2 + lax.rem(c + offset[2] + 2, 2)
+    )
+
+
+CHIPS = [(1, 1), (3, 3), (2, 0), (0, 2), (1, 3), (3, 1), (2, 2), (1, 0), (3, 0), (0, 1), (0, 3), (1, 2), (3, 2), (2, 1), (2, 3)]
+OFFSETS = [(a, b, c) for a, b in CHIPS for c in (0, 1)] + [(0, 0, 1)]
+
+
+def opposite(offset):
+    return tuple(-part for part in offset)
+
+
 def exchange_kernel(
     table_ref, cache_ref, out_ref, asked, asked_s, outgoing, ask_send, ask_recv, send_sem, recv_sem, local_sem
 ):
     me = lax.axis_index("dp")
     barrier = pltpu.get_barrier_semaphore()
-
-    def greet(i, carry):
-        pl.semaphore_signal(
-            barrier, inc=1, device_id={"dp": lax.rem(me + i, OWNERS)}, device_id_type=MESH
+    for offset in OFFSETS:
+        pl.semaphore_signal(barrier, inc=1, device_id={"dp": chip_at(offset)}, device_id_type=MESH)
+    pl.semaphore_wait(barrier, OWNERS - 1)
+
+    asks = []
+    for i, offset in enumerate(OFFSETS):
+        asks.append(
+            pltpu.make_async_remote_copy(
+                src_ref=table_ref,
+                dst_ref=asked.at[i],
+                send_sem=ask_send.at[i],
+                recv_sem=ask_recv.at[i],
+                device_id={"dp": chip_at(offset)},
+                device_id_type=MESH,
+            )
         )
-        return carry
-
-    lax.fori_loop(1, OWNERS, greet, 0)
-    pl.semaphore_wait(barrier, OWNERS - 1)
-
-    def ask(i):
-        peer = lax.rem(me + i, OWNERS)
-        return pltpu.make_async_remote_copy(
-            src_ref=table_ref,
-            dst_ref=asked.at[me],
-            send_sem=ask_send.at[peer],
-            recv_sem=ask_recv.at[me],
-            device_id={"dp": peer},
-            device_id_type=MESH,
-        )
-
-    def asked_by(i):
-        peer = lax.rem(me + i, OWNERS)
-        return pltpu.make_async_remote_copy(
-            src_ref=table_ref,
-            dst_ref=asked.at[peer],
-            send_sem=ask_send.at[peer],
-            recv_sem=ask_recv.at[peer],
-            device_id={"dp": peer},
-            device_id_type=MESH,
-        )
-
-    def start_ask(i, carry):
-        ask(i).start()
-        return carry
-
-    lax.fori_loop(1, OWNERS, start_ask, 0)
-    own = pltpu.make_async_copy(table_ref, asked.at[me], local_sem.at[0])
+        asks[-1].start()
+    own = pltpu.make_async_copy(table_ref, asked.at[OWNERS - 1], local_sem.at[0])
     own.start()
     own.wait()
-
-    def wait_ask(i, carry):
-        asked_by(i).wait()
-        return carry
-
-    lax.fori_loop(1, OWNERS, wait_ask, 0)
+    for ask in asks:
+        ask.wait()
     down = pltpu.make_async_copy(asked, asked_s, local_sem.at[1])
     down.start()
     down.wait()
 
-    def fill(peer):
+    def fill(slot, row):
         for k in range(CAP):
-            outgoing[peer, k] = cache_ref[asked_s[peer, 0, me * CAP + k]]
-
-    def send(i, carry):
-        peer = lax.rem(me + i, OWNERS)
-        fill(peer)
-        pltpu.make_async_remote_copy(
-            src_ref=outgoing.at[peer],
-            dst_ref=out_ref.at[me],
-            send_sem=send_sem.at[peer],
-            recv_sem=recv_sem.at[me],
-            device_id={"dp": peer},
-            device_id_type=MESH,
-        ).start()
-        return carry
-
-    lax.fori_loop(1, OWNERS, send, 0)
-    fill(me)
-    kept = pltpu.make_async_copy(outgoing.at[me], out_ref.at[me], local_sem.at[2])
+            outgoing[slot, k] = cache_ref[asked_s[row, 0, me * CAP + k]]
+
+    sends = []
+    for i, offset in enumerate(OFFSETS):
+        back = tuple((-p) % n for p, n in zip(offset, (4, 4, 2)))
+        fill(i, OFFSETS.index(back))
+        sends.append(
+            pltpu.make_async_remote_copy(
+                src_ref=outgoing.at[i],
+                dst_ref=out_ref.at[me],
+                send_sem=send_sem.at[i],
+                recv_sem=recv_sem.at[i],
+                device_id={"dp": chip_at(offset)},
+                device_id_type=MESH,
+            )
+        )
+        sends[-1].start()
+    fill(OWNERS - 1, OWNERS - 1)
+    kept = pltpu.make_async_copy(outgoing.at[OWNERS - 1], out_ref.at[me], local_sem.at[2])
     kept.start()
-
-    def finish(i, carry):
-        peer = lax.rem(me + i, OWNERS)
-        pltpu.make_async_remote_copy(
-            src_ref=outgoing.at[peer],
-            dst_ref=out_ref.at[peer],
-            send_sem=send_sem.at[peer],
-            recv_sem=recv_sem.at[peer],
-            device_id={"dp": peer},
-            device_id_type=MESH,
-        ).wait()
-        return carry
-
-    lax.fori_loop(1, OWNERS, finish, 0)
+    for send in sends:
+        send.wait()
     kept.wait()
 
 
@@ -383,6 +364,109 @@
     )(where, live, x, dy, w_in, w_out, fetched, *kept)
 
 
+HALF = (4 * HA + HA) // 2
+CHUNK = D // OWNERS
+
+
+def scatter_kernel(
+    part_ref, in_ref, out_ref, pair, mine, first, middle, second, pair_sem, first_sem, second_sem
+):
+    me = lax.axis_index("dp")
+    y, z, c = me // 8, lax.rem(me // 2, 4), lax.rem(me, 2)
+    steps = (1, 3, 2)
+    peers = [(0, 0, 1)] + [(s, 0, 0) for s in steps] + [(0, s, 0) for s in steps]
+    barrier = pltpu.get_barrier_semaphore()
+    for peer in peers:
+        pl.semaphore_signal(barrier, inc=1, device_id={"dp": chip_at(peer)}, device_id_type=MESH)
+    pl.semaphore_wait(barrier, len(peers))
+
+    def copy(src, dst, sems, offset):
+        made = pltpu.make_async_remote_copy(
+            src_ref=src,
+            dst_ref=dst,
+            send_sem=sems.at[0],
+            recv_sem=sems.at[1],
+            device_id={"dp": chip_at(offset)},
+            device_id_type=MESH,
+        )
+        made.start()
+        return made
+
+    cols = [pl.ds(h * HALF, HALF) for h in range(2)]
+    swaps = [
+        copy(part_ref.at[:, :, 1 - c, :, cols[h]], pair.at[h], pair_sem.at[h], (0, 0, 1)) for h in range(2)
+    ]
+    moves = [[], []]
+    for h in range(2):
+        swaps[h].wait()
+
+        def join(i, carry, h=h):
+            total = part_ref[i, :, c, :, h * HALF : (h + 1) * HALF].astype(F32) + pair[h, i].astype(F32)
+            mine[h, i] = total.astype(BF16)
+            return carry
+
+        lax.fori_loop(0, 4, join, 0)
+        for k, s in enumerate(steps):
+            offset = (s, 0, 0) if h == 0 else (0, s, 0)
+            at = lax.rem((z if h else y) + s, 4)
+            src = mine.at[h, :, at] if h else mine.at[h, at]
+            moves[h].append(copy(src, first.at[h, k], first_sem.at[h, k], offset))
+    later = [[], []]
+    for h in range(2):
+        for move in moves[h]:
+            move.wait()
+
+        def add(i, carry, h=h):
+            total = (mine[h, i, z] if h else mine[h, y, i]).astype(F32)
+            for k in range(3):
+                total += first[h, k, i].astype(F32)
+            middle[h, i] = total.astype(BF16)
+            return carry
+
+        lax.fori_loop(0, 4, add, 0)
+        for k, s in enumerate(steps):
+            offset = (0, s, 0) if h == 0 else (s, 0, 0)
+            at = lax.rem((y if h else z) + s, 4)
+            later[h].append(copy(middle.at[h, at], second.at[h, k], second_sem.at[h, k], offset))
+    for h in range(2):
+        for move in later[h]:
+            move.wait()
+        total = middle[h, y if h else z].astype(F32)
+        for k in range(3):
+            total += second[h, k].astype(F32)
+        if h == 0:
+            in_ref[:, :HALF] = total
+        else:
+            in_ref[:, HALF:] = total[:, : 4 * HA - HALF]
+            out_ref[...] = total[:, 4 * HA - HALF :]
+
+
+def summed(part):
+    return pl.pallas_call(
+        scatter_kernel,
+        out_shape=[
+            jax.ShapeDtypeStruct((CHUNK, 4 * HA), F32),
+            jax.ShapeDtypeStruct((CHUNK, HA), F32),
+        ],
+        in_specs=[VM],
+        out_specs=[VM, VM],
+        scratch_shapes=[
+            pltpu.VMEM((2, 4, 4, CHUNK, HALF), BF16),
+            pltpu.VMEM((2, 4, 4, CHUNK, HALF), BF16),
+            pltpu.VMEM((2, 3, 4, CHUNK, HALF), BF16),
+            pltpu.VMEM((2, 4, CHUNK, HALF), BF16),
+            pltpu.VMEM((2, 3, CHUNK, HALF), BF16),
+            pltpu.SemaphoreType.DMA((2, 2)),
+            pltpu.SemaphoreType.DMA((2, 3, 2)),
+            pltpu.SemaphoreType.DMA((2, 3, 2)),
+        ],
+        compiler_params=pltpu.CompilerParams(
+            collective_id=1, has_side_effects=True, vmem_limit_bytes=40 << 20
+        ),
+        name="scatter",
+    )(part)
+
+
 def passed_along(array, axis, by):
     peers = lax.axis_size(axis)
     pairs = [(i, i + by) for i in range(peers) if 0 <= i + by < peers]
@@ -422,13 +506,9 @@
         if step > 0:
             arriving = passed_along(dx, "section", -1)
             dy = jnp.where(section == step - 1, arriving, dy)
-    own_rows = lax.psum_scatter(
-        jnp.concatenate([dot(x_norm, dproj, 0, 0), dot(dy, gated, 0, 0)], axis=1).astype(BF16),
-        "dp",
-        scatter_dimension=0,
-        tiled=True,
-    ).astype(F32)
-    return (y[None], dx[None], own_rows[None, :, : 4 * HA], own_rows[None, :, 4 * HA :])
+    part = jnp.concatenate([dot(x_norm, dproj, 0, 0), dot(dy, gated, 0, 0)], axis=1).astype(BF16)
+    grad_in, grad_out = summed(part.reshape(4, 4, 2, CHUNK, 5 * HA))
+    return (y[None], dx[None], grad_in[None], grad_out[None])
 
 
 def solution(mesh):

time: 722 us -> 490 us (0.68)
  waiting for transfers between devices: 197 us -> 68.8 us
  Pallas kernels: 477 us -> 389 us
  between operations: 14.2 us -> 0.87 us
    reduce_scatter x1 -> x0, waiting for transfers between devices: 137 us -> none  [body(): lax.psum_scatter(jnp.concatenate([dot(x_norm, dproj, 0, 0), dot(dy, gated...]
    pallas_call x1, Pallas kernels: 336 us -> 217 us  [exchange(): pl.pallas_call(exchange_kernel, out_shape=jax.ShapeDtypeStruct((OWNERS, C...]
    pallas_call x0 -> x1, Pallas kernels: none -> 31.2 us  [summed(): pl.pallas_call(scatter_kernel, out_shape=[jax.ShapeDtypeStruct((CHUNK, 4...]
    ppermute x6, waiting for transfers between devices: 60 us -> 68.8 us  [passed_along(): return lax.ppermute(array, axis, pairs)]
  transfers between devices with their start and end apart: 7 -> 6, of which waited for: 7 -> 6; matrix products, arithmetic and copies ran while one was open for 0% -> 0% of each run, Pallas kernels for 0% -> 0%
where the time goes in v2:
time: 490 us; the launch traced here: 489 us
  Pallas kernels  389 us (79%)
  waiting for transfers between devices  68.8 us (14%)
  starting transfers between devices  16.6 us (3%)
  local copies, waits for them, and re-layouts  5.83 us (1%)
  other arithmetic  5.07 us (1%)
    pallas_call x1, Pallas kernels, exchange(): pl.pallas_call(exchange_kernel, out_shape=jax.ShapeDtypeStruct((OWNERS, C...  217 us
    pallas_call x4, Pallas kernels, backward(): pl.pallas_call(backward_kernel, out_shape=[jax.ShapeDtypeStruct((ROWS, D)...  74.7 us
    ppermute x6, waiting for transfers between devices, passed_along(): return lax.ppermute(array, axis, pairs)  68.8 us
    pallas_call x4, Pallas kernels, forward(): pl.pallas_call(partial(forward_kernel, keep), out_shape=outs, in_specs=[S...  66.3 us
    pallas_call x1, Pallas kernels, summed(): pl.pallas_call(scatter_kernel, out_shape=[jax.ShapeDtypeStruct((CHUNK, 4...  31.2 us
    ppermute x6, starting transfers between devices, passed_along(): return lax.ppermute(array, axis, pairs)  16.6 us
  transfers between devices with their start and end apart: 6, of which 6 were waited for; matrix products, arithmetic and copies ran while one was open for 0% of the time, Pallas kernels for 0%

profile of v2, /device:TPU:0, one launch (start us, length us, event | category | flops | bytes accessed | tf_op | source)
XLA Modules:
  0.0 489.1 jit_solution(9041397326742175450)
XLA Ops:
  0.6 0.5 broadcast.18
  1.2 1.3 reduce.3
  2.5 0.1 reshape.43
  2.6 0.2 convert_reduce_fusion
  2.8 0.8 broadcast_in_dim.34
  3.5 0.8 compare_select_fusion
  4.3 0.1 reshape.44.live_ref
  4.4 0.1 select_reduce_fusion
  4.5 2.2 copy-done.3
  6.7 216.9 %exchange.1 = bf16[32,2,128,1024]{3,2,1,0:T(8,128)(2,1)} custom-call(s32[1,128]{1,0:T(1,128)S(1)} %bitcast.19, bf16[16,128,1024]{2,1,0:T(8,128)(2,1)S(1)} %bitcast.16), custom_call_target="tpu_custom_call" | custom-call | tf_op jit(solution)/shard_map/exchange/pallas_call | solution.py:135
  223.5 0.0 copy-done.5
  223.5 15.4 %forward.3 = bf16[256,1024]{1,0:T(8,128)(2,1)S(1)} custom-call(s32[32]{0:T(128)S(1)} %multiply_add_fusion.where_ref, s32[32]{0:T(128)S(1)} %reshape.44.live_ref, bf16[256,1024]{1,0:T(8,128)(2,1)S(1)} %copy-done.5, bf16[1024,2048]{1,0:T(8,128)(2,1)} %bitcast.28, bf16[1024,512]{1,0:T(8,128)(2,1)} %bitcast.36, bf16[64,128,1024]{2,1,0:T(8,128)(2,1)} %bitcast.20), custom_call_target="tpu_custom_call" | custom-call | tf_op jit(solution)/shard_map/forward/pallas_call | solution.py:290
  238.9 3.4 collective-permute-start
  242.4 12.0 %collective-permute-done = bf16[256,1024]{1,0:T(8,128)(2,1)S(1)} collective-permute-done((bf16[256,1024]{1,0:T(8,128)(2,1)S(1)}, bf16[256,1024]{1,0:T(8,128)(2,1)S(1)}, u32[]{:S(2)}, u32[]{:S(2)}) %collective-permute-start) | collective-permute-done | bytes 524320 | tf_op jit(solution)/shard_map/ppermute | solution.py:473
  254.3 0.1 broadcast_select_fusion.2.x_ref
  254.4 15.4 %forward.4 = bf16[256,1024]{1,0:T(8,128)(2,1)S(1)} custom-call(s32[32]{0:T(128)S(1)} %multiply_add_fusion.where_ref, s32[32]{0:T(128)S(1)} %reshape.44.live_ref, bf16[256,1024]{1,0:T(8,128)(2,1)S(1)} %broadcast_select_fusion.2.x_ref, bf16[1024,2048]{1,0:T(8,128)(2,1)} %bitcast.29, bf16[1024,512]{1,0:T(8,128)(2,1)} %bitcast.37, bf16[64,128,1024]{2,1,0:T(8,128)(2,1)} %bitcast.21), custom_call_target="tpu_custom_call" | custom-call | tf_op jit(solution)/shard_map/forward/pallas_call | solution.py:290
  269.8 4.4 collective-permute-start.1
  274.2 11.1 %collective-permute-done.1 = bf16[256,1024]{1,0:T(8,128)(2,1)S(1)} collective-permute-done((bf16[256,1024]{1,0:T(8,128)(2,1)S(1)}, bf16[256,1024]{1,0:T(8,128)(2,1)S(1)}, u32[]{:S(2)}, u32[]{:S(2)}) %collective-permute-start.1) | collective-permute-done | bytes 524320 | tf_op jit(solution)/shard_map/ppermute | solution.py:473
  285.3 0.1 broadcast_select_fusion.4.x_ref
  285.4 15.4 %forward.5 = bf16[256,1024]{1,0:T(8,128)(2,1)S(1)} custom-call(s32[32]{0:T(128)S(1)} %multiply_add_fusion.where_ref, s32[32]{0:T(128)S(1)} %reshape.44.live_ref, bf16[256,1024]{1,0:T(8,128)(2,1)S(1)} %broadcast_select_fusion.4.x_ref, bf16[1024,2048]{1,0:T(8,128)(2,1)} %bitcast.30, bf16[1024,512]{1,0:T(8,128)(2,1)} %bitcast.38, bf16[64,128,1024]{2,1,0:T(8,128)(2,1)} %bitcast.22), custom_call_target="tpu_custom_call" | custom-call | tf_op jit(solution)/shard_map/forward/pallas_call | solution.py:290
  300.8 4.6 collective-permute-start.2
  305.4 10.0 %collective-permute-done.2 = bf16[256,1024]{1,0:T(8,128)(2,1)S(1)} collective-permute-done((bf16[256,1024]{1,0:T(8,128)(2,1)S(1)}, bf16[256,1024]{1,0:T(8,128)(2,1)S(1)}, u32[]{:S(2)}, u32[]{:S(2)}) %collective-permute-start.2) | collective-permute-done | bytes 524320 | tf_op jit(solution)/shard_map/ppermute | solution.py:473
  315.5 0.8 broadcast_select_fusion.5.x_ref
  316.3 20.1 %forward_keep.1 = (bf16[256,1024]{1,0:T(8,128)(2,1)}, bf16[256,1024]{1,0:T(8,128)(2,1)S(1)}, bf16[256,2048]{1,0:T(8,128)(2,1)}, f32[256,2048]{1,0:T(8,128)}, bf1...) custom-call(s32[32]{0:T(128)S(1)} %multiply_add_fusion.where_ref, ...), custom_call_target="tpu_custom_call" | custom-call | tf_op jit(solution)/shard_map/forward_keep/pallas_call | solution.py:290
  336.5 0.0 copy-start.1
  336.5 0.8 copy-done.1
  337.3 0.0 copy-done
  337.3 0.0 copy-done.4
  337.3 18.4 %backward.4 = (bf16[256,1024]{1,0:T(8,128)(2,1)S(1)}, bf16[256,2048]{1,0:T(8,128)(2,1)}) custom-call(s32[32]{0:T(128)S(1)} %multiply_add_fusion.where_ref, s32[32]{0:T(128)S(1)} %reshape.44.live_ref, bf16[256,1024]{1,0:T(8,128)(2,1)S(1)} %copy-done, bf16[256,1024]{1,0:T(8,128)(2,1)S(1)} %copy-done.4, bf16[1024,2048]{1,0:T(8,128)(2,1)} %bitcast.32, ...), custom_call_target="tpu_custom_call" | custom-call | tf_op jit(solution)/shard_map/backward/pallas_call | solution.py:349
  355.8 1.3 collective-permute-start.3
  357.1 13.2 %collective-permute-done.3 = bf16[256,1024]{1,0:T(8,128)(2,1)S(1)} collective-permute-done((bf16[256,1024]{1,0:T(8,128)(2,1)S(1)}, bf16[256,1024]{1,0:T(8,128)(2,1)S(1)}, u32[]{:S(2)}, u32[]{:S(2)}) %collective-permute-start.3) | collective-permute-done | bytes 524320 | tf_op jit(solution)/shard_map/ppermute | solution.py:473
  370.3 0.1 broadcast_select_fusion.3.dy_ref
  370.3 18.5 %backward.5 = (bf16[256,1024]{1,0:T(8,128)(2,1)S(1)}, bf16[256,2048]{1,0:T(8,128)(2,1)}) custom-call(s32[32]{0:T(128)S(1)} %multiply_add_fusion.where_ref, s32[32]{0:T(128)S(1)} %reshape.44.live_ref, bf16[256,1024]{1,0:T(8,128)(2,1)S(1)} %copy-done, bf16[256,1024]{1,0:T(8,128)(2,1)S(1)} %broadcast_select_fusion.3.dy_ref, bf16[1024,2048]{1,0:T(8,128)(2,1)} %bitcast.33, ...), custom_call_target="tpu_custom_call" | custom-call | tf_op jit(solution)/shard_map/backward/pallas_call | solution.py:349
  388.8 1.3 collective-permute-start.4
  390.1 11.8 %collective-permute-done.4 = bf16[256,1024]{1,0:T(8,128)(2,1)S(1)} collective-permute-done((bf16[256,1024]{1,0:T(8,128)(2,1)S(1)}, bf16[256,1024]{1,0:T(8,128)(2,1)S(1)}, u32[]{:S(2)}, u32[]{:S(2)}) %collective-permute-start.4) | collective-permute-done | bytes 524320 | tf_op jit(solution)/shard_map/ppermute | solution.py:473
  401.9 0.1 broadcast_select_fusion.1.dy_ref
  401.9 0.0 copy-start.2
  401.9 18.5 %backward.6 = (bf16[256,1024]{1,0:T(8,128)(2,1)S(1)}, bf16[256,2048]{1,0:T(8,128)(2,1)}) custom-call(s32[32]{0:T(128)S(1)} %multiply_add_fusion.where_ref, s32[32]{0:T(128)S(1)} %reshape.44.live_ref, bf16[256,1024]{1,0:T(8,128)(2,1)S(1)} %copy-done, bf16[256,1024]{1,0:T(8,128)(2,1)S(1)} %broadcast_select_fusion.1.dy_ref, bf16[1024,2048]{1,0:T(8,128)(2,1)} %bitcast.34, ...), custom_call_target="tpu_custom_call" | custom-call | tf_op jit(solution)/shard_map/backward/pallas_call | solution.py:349
  420.5 1.5 collective-permute-start.5
  422.0 10.7 %collective-permute-done.5 = bf16[256,1024]{1,0:T(8,128)(2,1)} collective-permute-done((bf16[256,1024]{1,0:T(8,128)(2,1)S(1)}, bf16[256,1024]{1,0:T(8,128)(2,1)}, u32[]{:S(2)}, u32[]{:S(2)}) %collective-permute-start.5) | collective-permute-done | bytes 524320 | tf_op jit(solution)/shard_map/ppermute | solution.py:473
  432.7 1.1 broadcast_select_fusion.dy_ref
  433.8 19.3 %backward.7 = (bf16[256,1024]{1,0:T(8,128)(2,1)}, bf16[256,2048]{1,0:T(8,128)(2,1)}) custom-call(s32[32]{0:T(128)S(1)} %multiply_add_fusion.where_ref, s32[32]{0:T(128)S(1)} %reshape.44.live_ref, bf16[256,1024]{1,0:T(8,128)(2,1)S(1)} %copy-done, bf16[256,1024]{1,0:T(8,128)(2,1)S(1)} %broadcast_select_fusion.dy_ref, bf16[1024,2048]{1,0:T(8,128)(2,1)} %bitcast.35, ...), custom_call_target="tpu_custom_call" | custom-call | tf_op jit(solution)/shard_map/backward/pallas_call | solution.py:349
  453.1 0.5 convolution_convert_fusion.1
  453.6 2.5 convolution_convert_fusion
  456.1 0.5 pad_maximum_fusion.part_ref
  456.6 31.2 %scatter.1 = (f32[32,2048]{1,0:T(8,128)S(1)}, f32[32,512]{1,0:T(8,128)S(1)}) custom-call(bf16[4,4,2,32,2560]{4,3,2,1,0:T(8,128)(2,1)S(1)} %pad_maximum_fusion.part_ref), custom_call_target="tpu_custom_call" | custom-call | tf_op jit(solution)/shard_map/scatter/pallas_call | solution.py:445
  487.8 0.7 copy.15
  488.5 0.6 copy.16
  (7 shorter events, 0.0 us)
Async XLA Ops:
  4.5 2.2 copy-start.3
  6.7 216.9 %copy-start.5 = (bf16[256,1024]{1,0:T(8,128)(2,1)S(1)}, bf16[256,1024]{1,0:T(8,128)(2,1)}, u32[]{:S(2)}) copy-start(bf16[256,1024]{1,0:T(8,128)(2,1)} %x_ref.1) | copy-start | bytes 1572868
  238.9 15.4 %collective-permute-start = (bf16[256,1024]{1,0:T(8,128)(2,1)S(1)}, bf16[256,1024]{1,0:T(8,128)(2,1)S(1)}, u32[]{:S(2)}, u32[]{:S(2)}) collective-permute-start(bf16[256,1024]{1,0:T(8,128)(2,1)S(1)} %forward.3), channel_id=1, source_target_pairs={{0,32},{32,64},{64,96},{1,33},{33,65},{65,97},{2,34},{34,66},{66,9... | collective-permute-start | bytes 1572872 | tf_op jit(solution)/shard_map/ppermute | solution.py:473
  269.8 15.5 %collective-permute-start.1 = (bf16[256,1024]{1,0:T(8,128)(2,1)S(1)}, bf16[256,1024]{1,0:T(8,128)(2,1)S(1)}, u32[]{:S(2)}, u32[]{:S(2)}) collective-permute-start(bf16[256,1024]{1,0:T(8,128)(2,1)S(1)} %forward.4), channel_id=1, source_target_pairs={{0,32},{32,64},{64,96},{1,33},{33,65},{65,97},{2,34},{34,66},{66,9... | collective-permute-start | bytes 1572872 | tf_op jit(solution)/shard_map/ppermute | solution.py:473
  300.8 14.7 %collective-permute-start.2 = (bf16[256,1024]{1,0:T(8,128)(2,1)S(1)}, bf16[256,1024]{1,0:T(8,128)(2,1)S(1)}, u32[]{:S(2)}, u32[]{:S(2)}) collective-permute-start(bf16[256,1024]{1,0:T(8,128)(2,1)S(1)} %forward.5), channel_id=1, source_target_pairs={{0,32},{32,64},{64,96},{1,33},{33,65},{65,97},{2,34},{34,66},{66,9... | collective-permute-start | bytes 1572872 | tf_op jit(solution)/shard_map/ppermute | solution.py:473
  316.3 21.0 %copy-start = (bf16[256,1024]{1,0:T(8,128)(2,1)S(1)}, bf16[256,1024]{1,0:T(8,128)(2,1)}, u32[]{:S(2)}) copy-start(bf16[256,1024]{1,0:T(8,128)(2,1)} %broadcast_select_fusion.5.x_ref) | copy-start | bytes 1572868
  316.3 21.0 %copy-start.4 = (bf16[256,1024]{1,0:T(8,128)(2,1)S(1)}, bf16[256,1024]{1,0:T(8,128)(2,1)}, u32[]{:S(2)}) copy-start(bf16[256,1024]{1,0:T(8,128)(2,1)} %dy_ref.1) | copy-start | bytes 1572868
  336.5 0.9 copy-start.1
  355.8 14.5 %collective-permute-start.3 = (bf16[256,1024]{1,0:T(8,128)(2,1)S(1)}, bf16[256,1024]{1,0:T(8,128)(2,1)S(1)}, u32[]{:S(2)}, u32[]{:S(2)}) collective-permute-start(bf16[256,1024]{1,0:T(8,128)(2,1)S(1)} %get-tuple-element.27), channel_id=1, source_target_pairs={{32,0},{64,32},{96,64},{33,1},{65,33},{97,65},{34,2},{66,34},{98,6... | collective-permute-start | bytes 1572872 | tf_op jit(solution)/shard_map/ppermute | solution.py:473
  388.8 13.1 %collective-permute-start.4 = (bf16[256,1024]{1,0:T(8,128)(2,1)S(1)}, bf16[256,1024]{1,0:T(8,128)(2,1)S(1)}, u32[]{:S(2)}, u32[]{:S(2)}) collective-permute-start(bf16[256,1024]{1,0:T(8,128)(2,1)S(1)} %get-tuple-element.28), channel_id=1, source_target_pairs={{32,0},{64,32},{96,64},{33,1},{65,33},{97,65},{34,2},{66,34},{98,6... | collective-permute-start | bytes 1572872 | tf_op jit(solution)/shard_map/ppermute | solution.py:473
  401.9 31.9 %copy-start.2 = (f32[256,512]{1,0:T(8,128)S(1)}, f32[256,512]{1,0:T(8,128)}, u32[]{:S(2)}) copy-start(f32[256,512]{1,0:T(8,128)} %copy-done.1) | copy-start | bytes 1572868
  420.5 12.2 %collective-permute-start.5 = (bf16[256,1024]{1,0:T(8,128)(2,1)S(1)}, bf16[256,1024]{1,0:T(8,128)(2,1)}, u32[]{:S(2)}, u32[]{:S(2)}) collective-permute-start(bf16[256,1024]{1,0:T(8,128)(2,1)S(1)} %get-tuple-element.29), channel_id=1, source_target_pairs={{32,0},{64,32},{96,64},{33,1},{65,33},{97,65},{34,2},{66,34},{98,6... | collective-permute-start | bytes 1572872 | tf_op jit(solution)/shard_map/ppermute | solution.py:473

commit v3 on v2

v3 whole, which is shorter than its diff:
```python
from functools import partial
import math

import jax
import jax.numpy as jnp
from jax import lax
from jax.experimental import pallas as pl
from jax.experimental.pallas import tpu as pltpu
from jax.sharding import PartitionSpec as P

HEADS = 4
EVT = 128
HBLK = 16
USERS = 2
ROWS = USERS * EVT
D = 1024
HA = 512
HD = HA // HEADS
CAP = 2
GROUP = 4
KEYS = HBLK * EVT
OWNERS = 32
epsilon = 1e-06
SCALE = 1.0 / math.sqrt(HD)
MESH = pl.DeviceIdType.MESH
F32 = jnp.float32
BF16 = jnp.bfloat16


def dot(a, b, ca=1, cb=0):
    return lax.dot_general(a, b, (((ca,), (cb,)), ((), ())), preferred_element_type=F32)


def normed(values):
    centred = values - jnp.mean(values, axis=-1, keepdims=True)
    inverse = lax.rsqrt(jnp.mean(centred * centred, axis=-1, keepdims=True) + epsilon)
    return centred * inverse, inverse


def norm_back(grad, value, inverse):
    return inverse * (
        grad
        - jnp.mean(grad, axis=-1, keepdims=True)
        - value * jnp.mean(grad * value, axis=-1, keepdims=True)
    )


def silu_parts(half):
    t = jnp.tanh(half)
    return half + half * t, 0.5 * ((1.0 + t) + half * (1.0 - t * t))


def chip_at(offset):
    me = lax.axis_index("dp")
    y, z, c = me // 8, lax.rem(me // 2, 4), lax.rem(me, 2)
    return (
        lax.rem(y + offset[0] + 4, 4) * 8 + lax.rem(z + offset[1] + 4, 4) * 2 + lax.rem(c + offset[2] + 2, 2)
    )


CHIPS = [(1, 1), (3, 3), (2, 0), (0, 2), (1, 3), (3, 1), (2, 2), (1, 0), (3, 0), (0, 1), (0, 3), (1, 2), (3, 2), (2, 1), (2, 3)]
OFFSETS = [(a, b, c) for a, b in CHIPS for c in (0, 1)] + [(0, 0, 1)]


def opposite(offset):
    return tuple(-part for part in offset)


def exchange_kernel(
    table_ref, cache_ref, out_ref, asked, asked_s, outgoing, ask_send, ask_recv, send_sem, recv_sem, local_sem
):
    me = lax.axis_index("dp")
    barrier = pltpu.get_barrier_semaphore()
    for offset in OFFSETS:
        pl.semaphore_signal(barrier, inc=1, device_id={"dp": chip_at(offset)}, device_id_type=MESH)
    pl.semaphore_wait(barrier, OWNERS - 1)

    asks = []
    for i, offset in enumerate(OFFSETS):
        asks.append(
            pltpu.make_async_remote_copy(
                src_ref=table_ref,
                dst_ref=asked.at[i],
                send_sem=ask_send.at[i],
                recv_sem=ask_recv.at[i],
                device_id={"dp": chip_at(offset)},
                device_id_type=MESH,
            )
        )
        asks[-1].start()
    own = pltpu.make_async_copy(table_ref, asked.at[OWNERS - 1], local_sem.at[0])
    own.start()
    own.wait()
    for ask in asks:
        ask.wait()
    down = pltpu.make_async_copy(asked, asked_s, local_sem.at[1])
    down.start()
    down.wait()

    def fill(slot, row):
        for k in range(CAP):
            outgoing[slot, k] = cache_ref[asked_s[row, 0, me * CAP + k]]

    sends = []
    for i, offset in enumerate(OFFSETS):
        back = tuple((-p) % n for p, n in zip(offset, (4, 4, 2)))
        fill(i, OFFSETS.index(back))
        sends.append(
            pltpu.make_async_remote_copy(
                src_ref=outgoing.at[i],
                dst_ref=out_ref.at[me],
                send_sem=send_sem.at[i],
                recv_sem=recv_sem.at[i],
                device_id={"dp": chip_at(offset)},
                device_id_type=MESH,
            )
        )
        sends[-1].start()
    fill(OWNERS - 1, OWNERS - 1)
    kept = pltpu.make_async_copy(outgoing.at[OWNERS - 1], out_ref.at[me], local_sem.at[2])
    kept.start()
    for send in sends:
        send.wait()
    kept.wait()


def exchange(table, cache):
    return pl.pallas_call(
        exchange_kernel,
        out_shape=jax.ShapeDtypeStruct((OWNERS, CAP, EVT, 2 * HA), BF16),
        in_specs=[pl.BlockSpec(memory_space=pltpu.VMEM)] * 2,
        out_specs=pl.BlockSpec(memory_space=pl.ANY),
        scratch_shapes=[
            pltpu.VMEM((OWNERS, 1, 128), jnp.int32),
            pltpu.SMEM((OWNERS, 1, 128), jnp.int32),
            pltpu.VMEM((OWNERS, CAP, EVT, 2 * HA), BF16),
            pltpu.SemaphoreType.DMA((OWNERS,)),
            pltpu.SemaphoreType.DMA((OWNERS,)),
            pltpu.SemaphoreType.DMA((OWNERS,)),
            pltpu.SemaphoreType.DMA((OWNERS,)),
            pltpu.SemaphoreType.DMA((3,)),
        ],
        compiler_params=pltpu.CompilerParams(
            collective_id=0, has_side_effects=True, vmem_limit_bytes=48 << 20
        ),
        name="exchange",
    )(table, cache)


VM = pl.BlockSpec(memory_space=pltpu.VMEM)
SM = pl.BlockSpec(memory_space=pltpu.SMEM)
ANY = pl.BlockSpec(memory_space=pl.ANY)


def columns(start):
    return pl.ds(pl.multiple_of(start, HD), HD)


def window_kernel(
    where_ref, live_ref, x_ref, cot_ref, w_in_ref, w_out_ref, fetched_ref,
    y_ref, dx_ref, x_norm_ref, dproj_ref, dy_ref, gated_ref,
    fetched, hist, x_now, x_value, x_rate, act, slope_in, slope, own_weights, mixed, value_ref, rate_ref, dmixed,
    x_arrived, dy_arrived, hist_sem, x_send, x_recv, dy_send, dy_recv,
):
    section = lax.axis_index("section")
    dp = lax.axis_index("dp")
    after, before = lax.rem(section + 1, 4), lax.rem(section + 3, 4)
    barrier = pltpu.get_barrier_semaphore()
    for peer in (before, after):
        pl.semaphore_signal(barrier, inc=1, device_id=(peer, dp), device_id_type=MESH)

    load = pltpu.make_async_copy(fetched_ref, fetched, hist_sem)
    load.start()
    pl.semaphore_wait(barrier, 2)

    def user_rows(user):
        return pl.ds(pl.multiple_of(user * EVT, EVT), EVT)

    def hop(src, dst, user, sends, recvs, peer):
        rows = user_rows(user)
        return pltpu.make_async_remote_copy(
            src_ref=src.at[rows],
            dst_ref=dst.at[rows],
            send_sem=sends.at[user],
            recv_sem=recvs.at[user],
            device_id=(peer, dp),
            device_id_type=MESH,
        )

    def x_hop(user):
        return hop(y_ref, x_arrived, user, x_send, x_recv, after)

    def dy_hop(user):
        return hop(dx_ref, dy_arrived, user, dy_send, dy_recv, before)

    row_of_block = lax.broadcasted_iota(jnp.int32, (EVT, HA), 0)
    causal = lax.broadcasted_iota(jnp.int32, (EVT, EVT), 1) <= lax.broadcasted_iota(
        jnp.int32, (EVT, EVT), 0
    )

    def inverse_count(user):
        total = live_ref[user * HBLK]
        for j in range(1, HBLK):
            total = total + live_ref[user * HBLK + j]
        return 1.0 / (jnp.full((EVT, 1), total, jnp.int32).astype(F32) + float(EVT))

    def history(user, group, start):
        blocks = pl.ds(user * HBLK + group * GROUP, GROUP)
        return hist[blocks, :, columns(start)].reshape(GROUP * EVT, HD)

    def place(r, carry):
        block = fetched[where_ref[r]]
        keep = (row_of_block < live_ref[r]).astype(F32).astype(BF16)
        hist[r, :, :HA] = block[:, :HA]
        hist[r, :, HA:] = block[:, HA:] * keep
        return carry

    @pl.when(section > 0)
    def _():
        load.wait()
        lax.fori_loop(0, USERS * HBLK, place, 0)

    def forward_user(user, carry):
        rows = user_rows(user)

        @pl.when(section == 0)
        def _():
            x_now[rows] = x_ref[rows]

        @pl.when(section > 0)
        def _():
            x_hop(user).wait_recv()
            x_now[rows] = x_arrived[rows]

        x = x_now[rows].astype(F32)
        normal, rate = normed(x)
        x_value[rows] = normal
        x_rate[rows] = jnp.broadcast_to(rate, (EVT, 128))
        x_norm = normal.astype(BF16)
        x_norm_ref[rows] = x_norm
        for c in range(4):
            part = slice(c * HA, (c + 1) * HA)
            made, rise = silu_parts(dot(x_norm, w_in_ref[:, part]) * 0.5)
            act[rows, part] = made.astype(BF16)
            slope_in[rows, part] = rise
        inverse = inverse_count(user)

        @pl.when((section == 0) & (user == 0))
        def _():
            load.wait()

        @pl.when(section == 0)
        def _():
            lax.fori_loop(user * HBLK, (user + 1) * HBLK, place, 0)

        def head_forward(head, carry):
            query = act[rows, columns(2 * HA + head * HD)]
            total = jnp.zeros((EVT, HD), F32)
            for group in range(HBLK // GROUP):
                half = dot(query, history(user, group, head * HD), 1, 1) * (0.5 * SCALE)
                weights = half + half * jnp.tanh(half)
                total += dot(weights.astype(BF16), history(user, group, HA + head * HD))
            half = dot(query, act[rows, columns(3 * HA + head * HD)], 1, 1) * (0.5 * SCALE)
            weights, rise = silu_parts(half)
            weights = jnp.where(causal, weights, 0.0).astype(BF16)
            total += dot(weights, act[rows, columns(HA + head * HD)])
            slope[user * HEADS + head, :, KEYS:] = jnp.where(causal, rise * SCALE, 0.0).astype(BF16)
            own_weights[user * HEADS + head] = weights
            mixed[rows, columns(head * HD)] = total * inverse
            return carry

        lax.fori_loop(0, HEADS, head_forward, 0)
        value, rate = normed(mixed[rows])
        gated = (value * act[rows, :HA].astype(F32)).astype(BF16)
        value_ref[rows] = value
        gated_ref[rows] = gated
        rate_ref[rows] = jnp.broadcast_to(rate, (EVT, 128))
        y_ref[rows] = (x + dot(gated, w_out_ref[...], 1, 1)).astype(BF16)

        @pl.when(section < 3)
        def _():
            x_hop(user).start()

        def head_slope(head, carry):
            query = act[rows, columns(2 * HA + head * HD)]
            for group in range(HBLK // GROUP):
                half = dot(query, history(user, group, head * HD), 1, 1) * (0.5 * SCALE)
                at = slice(group * GROUP * EVT, (group + 1) * GROUP * EVT)
                slope[user * HEADS + head, :, at] = (silu_parts(half)[1] * SCALE).astype(BF16)
            return carry

        lax.fori_loop(0, HEADS, head_slope, 0)
        return carry

    lax.fori_loop(0, USERS, forward_user, 0)

    def backward_user(user, carry):
        rows = user_rows(user)

        @pl.when(section == 3)
        def _():
            dy_ref[rows] = cot_ref[rows]

        @pl.when(section < 3)
        def _():
            dy_hop(user).wait_recv()
            dy_ref[rows] = dy_arrived[rows]

        dy = dy_ref[rows]
        dgated = dot(dy, w_out_ref[...])
        value = value_ref[rows]
        dproj_ref[rows, :HA] = (dgated * value * slope_in[rows, :HA]).astype(BF16)
        grad = norm_back(dgated * act[rows, :HA].astype(F32), value, rate_ref[rows, :1])
        dmixed[rows] = (grad * inverse_count(user)).astype(BF16)

        def head_back(head, carry):
            index = user * HEADS + head
            grad_mixed = dmixed[rows, columns(head * HD)]
            total = jnp.zeros((EVT, HD), F32)
            for group in range(HBLK // GROUP):
                rise = slope[index, :, group * GROUP * EVT : (group + 1) * GROUP * EVT].astype(F32)
                ds = (dot(grad_mixed, history(user, group, HA + head * HD), 1, 1) * rise).astype(BF16)
                total += dot(ds, history(user, group, head * HD))
            query = act[rows, columns(2 * HA + head * HD)]
            keys = act[rows, columns(3 * HA + head * HD)]
            values = act[rows, columns(HA + head * HD)]
            ds = (dot(grad_mixed, values, 1, 1) * slope[index, :, KEYS:].astype(F32)).astype(BF16)
            total += dot(ds, keys)
            dvalue = dot(own_weights[index], grad_mixed, 0, 0)
            dkey = dot(ds, query, 0, 0)
            for base, part in ((HA, dvalue), (2 * HA, total), (3 * HA, dkey)):
                at = columns(base + head * HD)
                dproj_ref[rows, at] = (part * slope_in[rows, at]).astype(BF16)
            return carry

        lax.fori_loop(0, HEADS, head_back, 0)
        dnorm = dot(dproj_ref[rows], w_in_ref[...], 1, 1)
        dx_ref[rows] = (
            dy.astype(F32) + norm_back(dnorm, x_value[rows], x_rate[rows, :1])
        ).astype(BF16)

        @pl.when(section > 0)
        def _():
            dy_hop(user).start()

        return carry

    lax.fori_loop(0, USERS, backward_user, 0)

    def finish(user, carry):
        @pl.when(section < 3)
        def _():
            x_hop(user).wait_send()

        @pl.when(section > 0)
        def _():
            dy_hop(user).wait_send()

        return carry

    lax.fori_loop(0, USERS, finish, 0)


def window(where, live, x, cot, w_in, w_out, fetched):
    heads = USERS * HEADS
    return pl.pallas_call(
        window_kernel,
        out_shape=[
            jax.ShapeDtypeStruct((ROWS, D), BF16),
            jax.ShapeDtypeStruct((ROWS, D), BF16),
            jax.ShapeDtypeStruct((ROWS, D), BF16),
            jax.ShapeDtypeStruct((ROWS, 4 * HA), BF16),
            jax.ShapeDtypeStruct((ROWS, D), BF16),
            jax.ShapeDtypeStruct((ROWS, HA), BF16),
        ],
        in_specs=[SM, SM, VM, VM, VM, VM, ANY],
        out_specs=[VM] * 6,
        scratch_shapes=[
            pltpu.VMEM(fetched.shape, BF16),
            pltpu.VMEM((USERS * HBLK, EVT, 2 * HA), BF16),
            pltpu.VMEM((ROWS, D), BF16),
            pltpu.VMEM((ROWS, D), F32),
            pltpu.VMEM((ROWS, 128), F32),
            pltpu.VMEM((ROWS, 4 * HA), BF16),
            pltpu.VMEM((ROWS, 4 * HA), F32),
            pltpu.VMEM((heads, EVT, KEYS + EVT), BF16),
            pltpu.VMEM((heads, EVT, EVT), BF16),
            pltpu.VMEM((ROWS, HA), F32),
            pltpu.VMEM((ROWS, HA), F32),
            pltpu.VMEM((ROWS, 128), F32),
            pltpu.VMEM((ROWS, HA), BF16),
            pltpu.VMEM((ROWS, D), BF16),
            pltpu.VMEM((ROWS, D), BF16),
            pltpu.SemaphoreType.DMA,
            pltpu.SemaphoreType.DMA((USERS,)),
            pltpu.SemaphoreType.DMA((USERS,)),
            pltpu.SemaphoreType.DMA((USERS,)),
            pltpu.SemaphoreType.DMA((USERS,)),
        ],
        compiler_params=pltpu.CompilerParams(
            collective_id=2, has_side_effects=True, vmem_limit_bytes=52 << 20
        ),
        name="window",
    )(where, live, x, cot, w_in, w_out, fetched)


HALF = (4 * HA + HA) // 2
CHUNK = D // OWNERS


def scatter_kernel(
    part_ref, in_ref, out_ref, pair, mine, first, middle, second, pair_sem, first_sem, second_sem
):
    me = lax.axis_index("dp")
    y, z, c = me // 8, lax.rem(me // 2, 4), lax.rem(me, 2)
    steps = (1, 3, 2)
    peers = [(0, 0, 1)] + [(s, 0, 0) for s in steps] + [(0, s, 0) for s in steps]
    barrier = pltpu.get_barrier_semaphore()
    for peer in peers:
        pl.semaphore_signal(barrier, inc=1, device_id={"dp": chip_at(peer)}, device_id_type=MESH)
    pl.semaphore_wait(barrier, len(peers))

    def copy(src, dst, sems, offset):
        made = pltpu.make_async_remote_copy(
            src_ref=src,
            dst_ref=dst,
            send_sem=sems.at[0],
            recv_sem=sems.at[1],
            device_id={"dp": chip_at(offset)},
            device_id_type=MESH,
        )
        made.start()
        return made

    cols = [pl.ds(h * HALF, HALF) for h in range(2)]
    swaps = [
        copy(part_ref.at[:, :, 1 - c, :, cols[h]], pair.at[h], pair_sem.at[h], (0, 0, 1)) for h in range(2)
    ]
    moves = [[], []]
    for h in range(2):
        swaps[h].wait()

        def join(i, carry, h=h):
            total = part_ref[i, :, c, :, h * HALF : (h + 1) * HALF].astype(F32) + pair[h, i].astype(F32)
            mine[h, i] = total.astype(BF16)
            return carry

        lax.fori_loop(0, 4, join, 0)
        for k, s in enumerate(steps):
            offset = (s, 0, 0) if h == 0 else (0, s, 0)
            at = lax.rem((z if h else y) + s, 4)
            src = mine.at[h, :, at] if h else mine.at[h, at]
            moves[h].append(copy(src, first.at[h, k], first_sem.at[h, k], offset))
    later = [[], []]
    for h in range(2):
        for move in moves[h]:
            move.wait()

        def add(i, carry, h=h):
            total = (mine[h, i, z] if h else mine[h, y, i]).astype(F32)
            for k in range(3):
                total += first[h, k, i].astype(F32)
            middle[h, i] = total.astype(BF16)
            return carry

        lax.fori_loop(0, 4, add, 0)
        for k, s in enumerate(steps):
            offset = (0, s, 0) if h == 0 else (s, 0, 0)
            at = lax.rem((y if h else z) + s, 4)
            later[h].append(copy(middle.at[h, at], second.at[h, k], second_sem.at[h, k], offset))
    for h in range(2):
        for move in later[h]:
            move.wait()
        total = middle[h, y if h else z].astype(F32)
        for k in range(3):
            total += second[h, k].astype(F32)
        if h == 0:
            in_ref[:, :HALF] = total
        else:
            in_ref[:, HALF:] = total[:, : 4 * HA - HALF]
            out_ref[...] = total[:, 4 * HA - HALF :]


def summed(part):
    return pl.pallas_call(
        scatter_kernel,
        out_shape=[
            jax.ShapeDtypeStruct((CHUNK, 4 * HA), F32),
            jax.ShapeDtypeStruct((CHUNK, HA), F32),
        ],
        in_specs=[VM],
        out_specs=[VM, VM],
        scratch_shapes=[
            pltpu.VMEM((2, 4, 4, CHUNK, HALF), BF16),
            pltpu.VMEM((2, 4, 4, CHUNK, HALF), BF16),
            pltpu.VMEM((2, 3, 4, CHUNK, HALF), BF16),
            pltpu.VMEM((2, 4, CHUNK, HALF), BF16),
            pltpu.VMEM((2, 3, CHUNK, HALF), BF16),
            pltpu.SemaphoreType.DMA((2, 2)),
            pltpu.SemaphoreType.DMA((2, 3, 2)),
            pltpu.SemaphoreType.DMA((2, 3, 2)),
        ],
        compiler_params=pltpu.CompilerParams(
            collective_id=1, has_side_effects=True, vmem_limit_bytes=40 << 20
        ),
        name="scatter",
    )(part)


def body(
    embeddings, in_proj, out_proj, hist_cache, hist_len, block_mask, block_owner, block_slot, cotangent
):
    w_in, w_out = in_proj[0], out_proj[0]
    requests = USERS * HBLK
    owner = block_owner.reshape(requests)
    order = jnp.arange(requests, dtype=jnp.int32)
    earlier = (owner[:, None] == owner[None, :]) & (order[None, :] < order[:, None])
    where = owner * CAP + jnp.sum(earlier.astype(jnp.int32), axis=1)
    names = jnp.arange(128, dtype=jnp.int32)
    table = jnp.sum(
        jnp.where(where[:, None] == names[None, :], block_slot.reshape(requests, 1), 0), axis=0
    )
    start = jnp.arange(HBLK, dtype=jnp.int32)[None, :] * EVT
    live = jnp.where(block_mask > 0, jnp.clip(hist_len[:, None] - start, 0, EVT), 0).reshape(requests)
    fetched = exchange(table.reshape(1, 128), hist_cache[0]).reshape(OWNERS * CAP, EVT, 2 * HA)

    y, dx, x_norm, dproj, dy, gated = window(
        where, live, embeddings, cotangent, w_in, w_out, fetched
    )
    part = jnp.concatenate([dot(x_norm, dproj, 0, 0), dot(dy, gated, 0, 0)], axis=1).astype(BF16)
    grad_in, grad_out = summed(part.reshape(4, 4, 2, CHUNK, 5 * HA))
    return (y[None], dx[None], grad_in[None], grad_out[None])


def solution(mesh):
    placed = (
        P("dp", None),
        P("section", None, None),
        P("section", None, None),
        P("section", "dp", None, None),
        P("dp"),
        P("dp", None),
        P("dp", None, None),
        P("dp", None),
        P("dp", None),
    )
    return jax.shard_map(
        body,
        mesh=mesh,
        in_specs=placed,
        out_specs=(
            P("section", "dp", None),
            P("section", "dp", None),
            P("section", "dp", None),
            P("section", "dp", None),
        ),
        check_vma=False,
    )
```

time: 490 us -> 376 us (0.77)
  waiting for transfers between devices: 68.8 us -> 0 us
  Pallas kernels: 389 us -> 361 us
  starting transfers between devices: 16.6 us -> 0 us
    ppermute x6 -> x0, waiting for transfers between devices: 68.8 us -> none  [passed_along(): return lax.ppermute(array, axis, pairs)]
    pallas_call x8 -> x1, Pallas kernels: 141 us -> 113 us  [window(): pl.pallas_call(window_kernel, out_shape=[jax.ShapeDtypeStruct((ROWS, D),...]
    ppermute x6 -> x0, starting transfers between devices: 16.6 us -> none  [passed_along(): return lax.ppermute(array, axis, pairs)]
  transfers between devices with their start and end apart: 6 -> 0, of which waited for: 6 -> 0; matrix products, arithmetic and copies ran while one was open for 0% -> 0% of each run, Pallas kernels for 0% -> 0%
where the time goes in v3:
time: 376 us; the launch traced here: 375 us
  Pallas kernels  361 us (96%)
  local copies, waits for them, and re-layouts  6.55 us (2%)
  matrix products  4.03 us (1%)
    pallas_call x1, Pallas kernels, exchange(): pl.pallas_call(exchange_kernel, out_shape=jax.ShapeDtypeStruct((OWNERS, C...  217 us
    pallas_call x1, Pallas kernels, window(): pl.pallas_call(window_kernel, out_shape=[jax.ShapeDtypeStruct((ROWS, D),...  113 us
    pallas_call x1, Pallas kernels, summed(): pl.pallas_call(scatter_kernel, out_shape=[jax.ShapeDtypeStruct((CHUNK, 4...  31.2 us

profile of v3, /device:TPU:0, one launch (start us, length us, event | category | flops | bytes accessed | tf_op | source)
XLA Modules:
  0.0 375.2 jit_solution(15456880242893978641)
XLA Ops:
  0.6 0.5 broadcast.18
  1.1 1.3 reduce.3
  2.5 0.1 reshape.43
  2.6 0.2 convert_reduce_fusion
  2.8 0.8 broadcast_in_dim.34
  3.5 0.1 select_reduce_fusion
  3.6 0.8 compare_select_fusion
  4.4 0.1 reshape.44.live_ref
  4.5 0.0 copy-start
  4.5 2.2 copy-done
  6.7 216.8 %exchange.1 = bf16[32,2,128,1024]{3,2,1,0:T(8,128)(2,1)} custom-call(s32[1,128]{1,0:T(1,128)S(1)} %bitcast.21, bf16[16,128,1024]{2,1,0:T(8,128)(2,1)S(1)} %bitcast.16), custom_call_target="tpu_custom_call" | custom-call | tf_op jit(solution)/shard_map/exchange/pallas_call | solution.py:128
  223.5 113.1 %window.1 = (bf16[256,1024]{1,0:T(8,128)(2,1)S(1)}, bf16[256,1024]{1,0:T(8,128)(2,1)S(1)}, bf16[256,1024]{1,0:T(8,128)(2,1)S(1)}, bf16[256,2048]{1,0:T(8,128)(2,...) custom-call(s32[32]{0:T(128)S(1)} %multiply_add_fusion.where_ref, s32[32]{0:T(128)S(1)} %reshape.44.live_ref, ...), custom_call_target="tpu_custom_call" | custom-call | tf_op jit(solution)/shard_map/window/pallas_call | solution.py:366
  336.6 1.5 convolution_convert_fusion.1
  338.1 2.5 convolution_convert_fusion
  340.6 0.5 pad_maximum_fusion.part_ref
  341.1 31.2 %scatter.1 = (f32[32,2048]{1,0:T(8,128)S(1)}, f32[32,512]{1,0:T(8,128)S(1)}) custom-call(bf16[4,4,2,32,2560]{4,3,2,1,0:T(8,128)(2,1)S(1)} %pad_maximum_fusion.part_ref), custom_call_target="tpu_custom_call" | custom-call | tf_op jit(solution)/shard_map/scatter/pallas_call | solution.py:485
  372.3 0.8 copy.17
  373.1 0.8 copy.18
  373.9 0.7 copy.19
  374.6 0.6 copy.20
  (2 shorter events, 0.0 us)
Async XLA Ops:
  4.5 2.2 copy-start

commit v4 on v3

--- a/solution.py
+++ b/solution.py
@@ -16,7 +16,6 @@
 D = 1024
 HA = 512
 HD = HA // HEADS
-CAP = 2
 GROUP = 4
 KEYS = HBLK * EVT
 OWNERS = 32
@@ -25,6 +24,9 @@
 MESH = pl.DeviceIdType.MESH
 F32 = jnp.float32
 BF16 = jnp.bfloat16
+VM = pl.BlockSpec(memory_space=pltpu.VMEM)
+SM = pl.BlockSpec(memory_space=pltpu.SMEM)
+ANY = pl.BlockSpec(memory_space=pl.ANY)
 
 
 def dot(a, b, ca=1, cb=0):
@@ -50,74 +52,112 @@
     return half + half * t, 0.5 * ((1.0 + t) + half * (1.0 - t * t))
 
 
+def place():
+    me = lax.axis_index("dp")
+    return me // 8, lax.rem(me // 2, 4), lax.rem(me, 2)
+
+
 def chip_at(offset):
-    me = lax.axis_index("dp")
-    y, z, c = me // 8, lax.rem(me // 2, 4), lax.rem(me, 2)
-    return (
-        lax.rem(y + offset[0] + 4, 4) * 8 + lax.rem(z + offset[1] + 4, 4) * 2 + lax.rem(c + offset[2] + 2, 2)
-    )
-
-
-CHIPS = [(1, 1), (3, 3), (2, 0), (0, 2), (1, 3), (3, 1), (2, 2), (1, 0), (3, 0), (0, 1), (0, 3), (1, 2), (3, 2), (2, 1), (2, 3)]
-OFFSETS = [(a, b, c) for a, b in CHIPS for c in (0, 1)] + [(0, 0, 1)]
-
-
-def opposite(offset):
-    return tuple(-part for part in offset)
+    y, z, c = place()
+    return lax.rem(y + offset[0], 4) * 8 + lax.rem(z + offset[1], 4) * 2 + lax.rem(c + offset[2], 2)
+
+
+ORDER = (
+    [(1, 0), (3, 0), (2, 0), (1, 1), (3, 3), (2, 1), (2, 3), (1, 3), (3, 1), (2, 2), (1, 2), (3, 2), (0, 1), (0, 3), (0, 2)],
+    [(0, 1), (0, 3), (0, 2), (1, 2), (3, 2), (1, 1), (3, 3), (2, 2), (1, 3), (3, 1), (2, 1), (2, 3), (1, 0), (3, 0), (2, 0)],
+)
+PEERS = [(a, b, c) for a in range(4) for b in range(4) for c in range(2)][1:]
+SLOTS = 4
+BLOCK = (EVT, 2 * HA)
+
+
+def name_of(y, z, c):
+    return y * 8 + z * 2 + c
+
+
+def reverse_name(y, z, c):
+    return lax.rem(4 - y, 4) * 8 + lax.rem(4 - z, 4) * 2 + c
+
+
+def to_peer(src, dst, send_sem, recv_sem, peer):
+    return pltpu.make_async_remote_copy(
+        src_ref=src,
+        dst_ref=dst,
+        send_sem=send_sem,
+        recv_sem=recv_sem,
+        device_id={"dp": peer},
+        device_id_type=MESH,
+    )
+
+
+def greet_all(peers):
+    barrier = pltpu.get_barrier_semaphore()
+    for peer in peers:
+        pl.semaphore_signal(barrier, inc=1, device_id={"dp": chip_at(peer)}, device_id_type=MESH)
+    pl.semaphore_wait(barrier, len(peers))
+
+
+def both_caches(cache_ref, cache, swap_sem, local_sem):
+    core = lax.rem(lax.axis_index("dp"), 2)
+    mine = cache.at[pl.ds(core * HBLK, HBLK)]
+    swap = to_peer(cache_ref, mine, swap_sem.at[0], swap_sem.at[1], chip_at((0, 0, 1)))
+    own = pltpu.make_async_copy(cache_ref, mine, local_sem)
+    swap.start()
+    own.start()
+    return swap, own
+
+
+def ordered(i, core):
+    (y0, z0), (y1, z1) = ORDER[0][i], ORDER[1][i]
+    return y0 + core * (y1 - y0), z0 + core * (z1 - z0)
 
 
 def exchange_kernel(
-    table_ref, cache_ref, out_ref, asked, asked_s, outgoing, ask_send, ask_recv, send_sem, recv_sem, local_sem
+    table_ref, cache_ref, out_ref, asked_ref, cache, asked_s, outgoing, own_blocks,
+    swap_sem, ask_send, ask_recv, one_send, one_recv, two_send, two_recv, local_sem,
 ):
-    me = lax.axis_index("dp")
-    barrier = pltpu.get_barrier_semaphore()
-    for offset in OFFSETS:
-        pl.semaphore_signal(barrier, inc=1, device_id={"dp": chip_at(offset)}, device_id_type=MESH)
-    pl.semaphore_wait(barrier, OWNERS - 1)
-
+    y, z, core = place()
+    chip = y * 4 + z
+    greet_all(PEERS)
+    swap, own = both_caches(cache_ref, cache, swap_sem, local_sem.at[0])
     asks = []
-    for i, offset in enumerate(OFFSETS):
+    for peer in PEERS:
+        name = name_of(*peer)
         asks.append(
-            pltpu.make_async_remote_copy(
-                src_ref=table_ref,
-                dst_ref=asked.at[i],
-                send_sem=ask_send.at[i],
-                recv_sem=ask_recv.at[i],
-                device_id={"dp": chip_at(offset)},
-                device_id_type=MESH,
-            )
+            to_peer(table_ref, asked_ref.at[name], ask_send.at[name], ask_recv.at[name], chip_at(peer))
         )
         asks[-1].start()
-    own = pltpu.make_async_copy(table_ref, asked.at[OWNERS - 1], local_sem.at[0])
-    own.start()
-    own.wait()
+    row = pltpu.make_async_copy(table_ref, asked_ref.at[0], local_sem.at[1])
+    row.start()
+    row.wait()
     for ask in asks:
         ask.wait()
-    down = pltpu.make_async_copy(asked, asked_s, local_sem.at[1])
+    down = pltpu.make_async_copy(asked_ref, asked_s, local_sem.at[2])
     down.start()
     down.wait()
-
-    def fill(slot, row):
-        for k in range(CAP):
-            outgoing[slot, k] = cache_ref[asked_s[row, 0, me * CAP + k]]
+    swap.wait()
+    own.wait()
 
     sends = []
-    for i, offset in enumerate(OFFSETS):
-        back = tuple((-p) % n for p, n in zip(offset, (4, 4, 2)))
-        fill(i, OFFSETS.index(back))
-        sends.append(
-            pltpu.make_async_remote_copy(
-                src_ref=outgoing.at[i],
-                dst_ref=out_ref.at[me],
-                send_sem=send_sem.at[i],
-                recv_sem=recv_sem.at[i],
-                device_id={"dp": chip_at(offset)},
-                device_id_type=MESH,
-            )
-        )
-        sends[-1].start()
-    fill(OWNERS - 1, OWNERS - 1)
-    kept = pltpu.make_async_copy(outgoing.at[OWNERS - 1], out_ref.at[me], local_sem.at[2])
+    for i in range(15):
+        dy, dz = ordered(i, core)
+        name = dy * 4 + dz
+        for dc in range(2):
+            row = reverse_name(dy, dz, dc)
+            if dc == 0:
+                outgoing[i, 1] = cache[asked_s[row, 0, chip * SLOTS + 1]]
+                outgoing[i, 2] = cache[asked_s[row, 0, chip * SLOTS + 2]]
+                src, dst = outgoing.at[i, pl.ds(1, 2)], out_ref.at[chip, pl.ds(1, 2)]
+                sems = two_send.at[name], two_recv.at[name]
+            else:
+                outgoing[i, 0] = cache[asked_s[row, 0, chip * SLOTS]]
+                src, dst = outgoing.at[i, 0], out_ref.at[chip, 0]
+                sems = one_send.at[name], one_recv.at[name]
+            sends.append(to_peer(src, dst, *sems, chip_at((dy, dz, dc))))
+            sends[-1].start()
+    for k in range(SLOTS):
+        own_blocks[k] = cache[asked_s[0, 0, chip * SLOTS + k]]
+    kept = pltpu.make_async_copy(own_blocks, out_ref.at[chip], local_sem.at[3])
     kept.start()
     for send in sends:
         send.wait()
@@ -127,29 +167,77 @@
 def exchange(table, cache):
     return pl.pallas_call(
         exchange_kernel,
-        out_shape=jax.ShapeDtypeStruct((OWNERS, CAP, EVT, 2 * HA), BF16),
-        in_specs=[pl.BlockSpec(memory_space=pltpu.VMEM)] * 2,
-        out_specs=pl.BlockSpec(memory_space=pl.ANY),
+        out_shape=[
+            jax.ShapeDtypeStruct((OWNERS // 2, SLOTS) + BLOCK, BF16),
+            jax.ShapeDtypeStruct((OWNERS, 1, 128), jnp.int32),
+        ],
+        in_specs=[VM, ANY],
+        out_specs=[ANY, VM],
         scratch_shapes=[
-            pltpu.VMEM((OWNERS, 1, 128), jnp.int32),
+            pltpu.VMEM((2 * HBLK,) + BLOCK, BF16),
             pltpu.SMEM((OWNERS, 1, 128), jnp.int32),
-            pltpu.VMEM((OWNERS, CAP, EVT, 2 * HA), BF16),
+            pltpu.VMEM((15, 3) + BLOCK, BF16),
+            pltpu.VMEM((SLOTS,) + BLOCK, BF16),
+            pltpu.SemaphoreType.DMA((2,)),
             pltpu.SemaphoreType.DMA((OWNERS,)),
             pltpu.SemaphoreType.DMA((OWNERS,)),
-            pltpu.SemaphoreType.DMA((OWNERS,)),
-            pltpu.SemaphoreType.DMA((OWNERS,)),
-            pltpu.SemaphoreType.DMA((3,)),
+            pltpu.SemaphoreType.DMA((16,)),
+            pltpu.SemaphoreType.DMA((16,)),
+            pltpu.SemaphoreType.DMA((16,)),
+            pltpu.SemaphoreType.DMA((16,)),
+            pltpu.SemaphoreType.DMA((4,)),
         ],
         compiler_params=pltpu.CompilerParams(
-            collective_id=0, has_side_effects=True, vmem_limit_bytes=48 << 20
+            collective_id=0, has_side_effects=True, vmem_limit_bytes=40 << 20
         ),
         name="exchange",
     )(table, cache)
 
 
-VM = pl.BlockSpec(memory_space=pltpu.VMEM)
-SM = pl.BlockSpec(memory_space=pltpu.SMEM)
-ANY = pl.BlockSpec(memory_space=pl.ANY)
+def fourth_kernel(
+    asked_ref, cache_ref, got_ref, out_ref, cache, outgoing, swap_sem, send_sem, recv_sem, local_sem
+):
+    del got_ref
+    y, z, core = place()
+    chip = y * 4 + z
+    peers = [(a, b, 0) for a, b in ORDER[0]]
+    greet_all(peers + [(0, 0, 1)])
+    swap, own = both_caches(cache_ref, cache, swap_sem, local_sem)
+    swap.wait()
+    own.wait()
+    sends = []
+    for i, (dy, dz, _) in enumerate(peers):
+        outgoing[i] = cache[asked_ref[reverse_name(dy, dz, 0), 0, chip * SLOTS + 3]]
+        sends.append(
+            to_peer(
+                outgoing.at[i], out_ref.at[chip, 3], send_sem.at[i], recv_sem.at[i], chip_at((dy, dz, 0))
+            )
+        )
+        sends[-1].start()
+    for send in sends:
+        send.wait()
+
+
+def fourth(asked, cache, got):
+    return pl.pallas_call(
+        fourth_kernel,
+        out_shape=jax.ShapeDtypeStruct(got.shape, BF16),
+        in_specs=[SM, ANY, ANY],
+        out_specs=ANY,
+        scratch_shapes=[
+            pltpu.VMEM((2 * HBLK,) + BLOCK, BF16),
+            pltpu.VMEM((15,) + BLOCK, BF16),
+            pltpu.SemaphoreType.DMA((2,)),
+            pltpu.SemaphoreType.DMA((15,)),
+            pltpu.SemaphoreType.DMA((15,)),
+            pltpu.SemaphoreType.DMA,
+        ],
+        input_output_aliases={2: 0},
+        compiler_params=pltpu.CompilerParams(
+            collective_id=3, has_side_effects=True, vmem_limit_bytes=24 << 20
+        ),
+        name="fourth",
+    )(asked, cache, got)
 
 
 def columns(start):
@@ -208,7 +296,7 @@
         blocks = pl.ds(user * HBLK + group * GROUP, GROUP)
         return hist[blocks, :, columns(start)].reshape(GROUP * EVT, HD)
 
-    def place(r, carry):
+    def settle(r, carry):
         block = fetched[where_ref[r]]
         keep = (row_of_block < live_ref[r]).astype(F32).astype(BF16)
         hist[r, :, :HA] = block[:, :HA]
@@ -218,7 +306,7 @@
     @pl.when(section > 0)
     def _():
         load.wait()
-        lax.fori_loop(0, USERS * HBLK, place, 0)
+        lax.fori_loop(0, USERS * HBLK, settle, 0)
 
     def forward_user(user, carry):
         rows = user_rows(user)
@@ -251,7 +339,7 @@
 
         @pl.when(section == 0)
         def _():
-            lax.fori_loop(user * HBLK, (user + 1) * HBLK, place, 0)
+            lax.fori_loop(user * HBLK, (user + 1) * HBLK, settle, 0)
 
         def head_forward(head, carry):
             query = act[rows, columns(2 * HA + head * HD)]
@@ -512,18 +600,33 @@
 ):
     w_in, w_out = in_proj[0], out_proj[0]
     requests = USERS * HBLK
-    owner = block_owner.reshape(requests)
+    start = jnp.arange(HBLK, dtype=jnp.int32)[None, :] * EVT
+    live = jnp.where(block_mask > 0, jnp.clip(hist_len[:, None] - start, 0, EVT), 0).reshape(requests)
+    wanted = live > 0
+    owner = jnp.where(wanted, block_owner.reshape(requests), -2)
     order = jnp.arange(requests, dtype=jnp.int32)
     earlier = (owner[:, None] == owner[None, :]) & (order[None, :] < order[:, None])
-    where = owner * CAP + jnp.sum(earlier.astype(jnp.int32), axis=1)
+    rank = jnp.sum(earlier.astype(jnp.int32), axis=1)
+    beside = jnp.sum(((owner ^ 1)[:, None] == owner[None, :]).astype(jnp.int32), axis=1)
+    me = lax.axis_index("dp")
+    chip, core, side = owner // 2, owner % 2, me % 2
+    slot = jnp.where(rank == 0, jnp.where(core == side, 1, 0), jnp.where((core == 1) & (beside == 2), 3, 2))
+    where = jnp.where(wanted, chip * SLOTS + slot, me // 2 * SLOTS)
     names = jnp.arange(128, dtype=jnp.int32)
+    number = core * HBLK + block_slot.reshape(requests)
+    late = wanted & (slot == 3) & (chip != me // 2)
+    here = (where[:, None] == names[None, :]) & wanted[:, None]
     table = jnp.sum(
-        jnp.where(where[:, None] == names[None, :], block_slot.reshape(requests, 1), 0), axis=0
-    )
-    start = jnp.arange(HBLK, dtype=jnp.int32)[None, :] * EVT
-    live = jnp.where(block_mask > 0, jnp.clip(hist_len[:, None] - start, 0, EVT), 0).reshape(requests)
-    fetched = exchange(table.reshape(1, 128), hist_cache[0]).reshape(OWNERS * CAP, EVT, 2 * HA)
-
+        jnp.where(here, number[:, None], 0)
+        + jnp.where(late[:, None] & (names[None, :] == 127), 1, 0),
+        axis=0,
+    )
+    cache = hist_cache[0]
+    got, asked = exchange(table.reshape(1, 128), cache)
+    got = lax.cond(
+        jnp.max(asked[:, 0, 127]) > 0, lambda g: fourth(asked, cache, g), lambda g: g, got
+    )
+    fetched = got.reshape(OWNERS // 2 * SLOTS, EVT, 2 * HA)
     y, dx, x_norm, dproj, dy, gated = window(
         where, live, embeddings, cotangent, w_in, w_out, fetched
     )

time: 376 us -> 377 us (level)
    pallas_call x1 -> x2, Pallas kernels: 217 us -> 219 us  [the longest x1 153 us: exchange(): pl.pallas_call(exchange_kernel, out_shape=[jax.ShapeDtypeStruct((OWNERS /...]
where the time goes in v4:
time: 377 us; the launch traced here: 376 us
  Pallas kernels  363 us (96%)
  local copies, waits for them, and re-layouts  4.36 us (1%)
  matrix products  4.02 us (1%)
    pallas_call x1, Pallas kernels, exchange(): pl.pallas_call(exchange_kernel, out_shape=[jax.ShapeDtypeStruct((OWNERS /...  153 us
    pallas_call x1, Pallas kernels, window(): pl.pallas_call(window_kernel, out_shape=[jax.ShapeDtypeStruct((ROWS, D),...  110 us
    pallas_call x1, Pallas kernels, fourth(): pl.pallas_call(fourth_kernel, out_shape=jax.ShapeDtypeStruct(got.shape, B...  66.5 us
    pallas_call x1, Pallas kernels, summed(): pl.pallas_call(scatter_kernel, out_shape=[jax.ShapeDtypeStruct((CHUNK, 4...  33 us

profile of v4, /device:TPU:0, one launch (start us, length us, event | category | flops | bytes accessed | tf_op | source)
XLA Modules:
  0.0 376.0 jit_solution(12768972508059260329)
XLA Ops:
  0.6 0.5 broadcast.275
  1.2 1.3 reduce.4
  2.5 0.1 reshape.143
  2.6 0.8 reshape.144
  3.4 0.8 compare_select_fusion.2
  4.1 0.1 reshape.142.live_ref
  4.2 0.2 convert_reduce_fusion
  4.4 0.1 add_reduce_fusion
  4.5 152.8 %exchange.1 = (bf16[16,4,128,1024]{3,2,1,0:T(8,128)(2,1)}, s32[32,1,128]{2,1,0:T(1,128)S(1)}) custom-call(s32[1,128]{1,0:T(1,128)S(1)} %bitcast.21, bf16[16,128,1024]{2,1,0:T(8,128)(2,1)} %bitcast.25), custom_call_target="tpu_custom_call" | custom-call | tf_op jit(solution)/shard_map/exchange/pallas_call | solution.py:168
  157.4 0.7 slice_reduce_fusion
  158.8 66.6 %conditional.1 = (bf16[64,128,1024]{2,1,0:T(8,128)(2,1)}) conditional(s32[]{:T(128)} %convert_element_type.13, bf16[16,4,128,1024]{3,2,1,0:T(8,128)(2,1)} %get-tuple-element.34, (s32[32,1,128]{2,1,0:T(1,128)S(1)}, bf16[16,128,1024]{2,1,0:T(8,128)(2,1)}, bf16[16,4,128,1024]{3,2,1,0:T(8,128)(2,1)}) %tuple.40), branch_computations={%region_4.5_spmd, %region_5.6_spmd} | conditional | bytes 8 | solution.py:626
  158.8 66.5 %fourth.1 = bf16[16,4,128,1024]{3,2,1,0:T(8,128)(2,1)} custom-call(s32[32,1,128]{2,1,0:T(1,128)S(1)} %get-tuple-element.16.asked_ref, bf16[16,128,1024]{2,1,0:T(8,128)(2,1)} %get-tuple-element.17.cache_ref, bf16[16,4,128,1024]{3,2,1,0:T(8,128)(2,1)} %get-tuple-element.18.got_ref), custom_call_target="tpu_custom_call", output_to_operand_aliasing={{}: (2, {})} | custom-call | tf_op jit(solution)/shard_map/cond/branch_1_fun/fourth/pallas_call | solution.py:222
  225.3 110.2 %window.1 = (bf16[256,1024]{1,0:T(8,128)(2,1)S(1)}, bf16[256,1024]{1,0:T(8,128)(2,1)S(1)}, bf16[256,1024]{1,0:T(8,128)(2,1)S(1)}, bf16[256,2048]{1,0:T(8,128)(2,...) custom-call(s32[32]{0:T(128)S(1)} %get-tuple-element.54.where_ref, s32[32]{0:T(128)S(1)} %reshape.142.live_ref, ...), custom_call_target="tpu_custom_call" | custom-call | tf_op jit(solution)/shard_map/window/pallas_call | solution.py:454
  335.5 1.5 convolution_convert_fusion.1
  337.0 2.5 convolution_convert_fusion
  339.6 0.5 pad_maximum_fusion.part_ref
  340.1 33.0 %scatter.1 = (f32[32,2048]{1,0:T(8,128)S(1)}, f32[32,512]{1,0:T(8,128)S(1)}) custom-call(bf16[4,4,2,32,2560]{4,3,2,1,0:T(8,128)(2,1)S(1)} %pad_maximum_fusion.part_ref), custom_call_target="tpu_custom_call" | custom-call | tf_op jit(solution)/shard_map/scatter/pallas_call | solution.py:573
  373.1 0.8 copy.23
  373.9 0.8 copy.24
  374.7 0.7 copy.25
  375.4 0.6 copy.26
  (5 shorter events, 0.0 us)

commit v5 on v4

--- a/solution.py
+++ b/solution.py
@@ -16,7 +16,7 @@
 D = 1024
 HA = 512
 HD = HA // HEADS
-GROUP = 4
+GROUP = 8
 KEYS = HBLK * EVT
 OWNERS = 32
 epsilon = 1e-06
@@ -247,7 +247,7 @@
 def window_kernel(
     where_ref, live_ref, x_ref, cot_ref, w_in_ref, w_out_ref, fetched_ref,
     y_ref, dx_ref, x_norm_ref, dproj_ref, dy_ref, gated_ref,
-    fetched, hist, x_now, x_value, x_rate, act, slope_in, slope, own_weights, mixed, value_ref, rate_ref, dmixed,
+    fetched, hist, w_in_t, x_now, x_value, x_rate, act, slope_in, slope, own_weights, mixed, value_ref, rate_ref, dmixed,
     x_arrived, dy_arrived, hist_sem, x_send, x_recv, dy_send, dy_recv,
 ):
     section = lax.axis_index("section")
@@ -303,8 +303,13 @@
         hist[r, :, HA:] = block[:, HA:] * keep
         return carry
 
+    def turn_w_in():
+        for k in range(0, 4 * HA, HD):
+            w_in_t[k : k + HD] = w_in_ref[:, k : k + HD].T
+
     @pl.when(section > 0)
     def _():
+        turn_w_in()
         load.wait()
         lax.fori_loop(0, USERS * HBLK, settle, 0)
 
@@ -346,7 +351,9 @@
             total = jnp.zeros((EVT, HD), F32)
             for group in range(HBLK // GROUP):
                 half = dot(query, history(user, group, head * HD), 1, 1) * (0.5 * SCALE)
-                weights = half + half * jnp.tanh(half)
+                weights, rise = silu_parts(half)
+                at = slice(group * GROUP * EVT, (group + 1) * GROUP * EVT)
+                slope[user * HEADS + head, :, at] = (rise * SCALE).astype(BF16)
                 total += dot(weights.astype(BF16), history(user, group, HA + head * HD))
             half = dot(query, act[rows, columns(3 * HA + head * HD)], 1, 1) * (0.5 * SCALE)
             weights, rise = silu_parts(half)
@@ -357,7 +364,7 @@
             mixed[rows, columns(head * HD)] = total * inverse
             return carry
 
-        lax.fori_loop(0, HEADS, head_forward, 0)
+        lax.fori_loop(0, HEADS, head_forward, 0, unroll=True)
         value, rate = normed(mixed[rows])
         gated = (value * act[rows, :HA].astype(F32)).astype(BF16)
         value_ref[rows] = value
@@ -369,18 +376,13 @@
         def _():
             x_hop(user).start()
 
-        def head_slope(head, carry):
-            query = act[rows, columns(2 * HA + head * HD)]
-            for group in range(HBLK // GROUP):
-                half = dot(query, history(user, group, head * HD), 1, 1) * (0.5 * SCALE)
-                at = slice(group * GROUP * EVT, (group + 1) * GROUP * EVT)
-                slope[user * HEADS + head, :, at] = (silu_parts(half)[1] * SCALE).astype(BF16)
-            return carry
-
-        lax.fori_loop(0, HEADS, head_slope, 0)
         return carry
 
     lax.fori_loop(0, USERS, forward_user, 0)
+
+    @pl.when(section == 0)
+    def _():
+        turn_w_in()
 
     def backward_user(user, carry):
         rows = user_rows(user)
@@ -421,8 +423,8 @@
                 dproj_ref[rows, at] = (part * slope_in[rows, at]).astype(BF16)
             return carry
 
-        lax.fori_loop(0, HEADS, head_back, 0)
-        dnorm = dot(dproj_ref[rows], w_in_ref[...], 1, 1)
+        lax.fori_loop(0, HEADS, head_back, 0, unroll=True)
+        dnorm = dot(dproj_ref[rows], w_in_t[...])
         dx_ref[rows] = (
             dy.astype(F32) + norm_back(dnorm, x_value[rows], x_rate[rows, :1])
         ).astype(BF16)
@@ -466,6 +468,7 @@
         scratch_shapes=[
             pltpu.VMEM(fetched.shape, BF16),
             pltpu.VMEM((USERS * HBLK, EVT, 2 * HA), BF16),
+            pltpu.VMEM((4 * HA, D), BF16),
             pltpu.VMEM((ROWS, D), BF16),
             pltpu.VMEM((ROWS, D), F32),
             pltpu.VMEM((ROWS, 128), F32),
@@ -486,113 +489,151 @@
             pltpu.SemaphoreType.DMA((USERS,)),
         ],
         compiler_params=pltpu.CompilerParams(
-            collective_id=2, has_side_effects=True, vmem_limit_bytes=52 << 20
+            collective_id=2, has_side_effects=True, vmem_limit_bytes=56 << 20
         ),
         name="window",
     )(where, live, x, cot, w_in, w_out, fetched)
 
 
-HALF = (4 * HA + HA) // 2
+PARTS = 4
+WIDE = (4 * HA + HA) // PARTS
+LAST = 4 * HA - (PARTS - 1) * WIDE
 CHUNK = D // OWNERS
 
 
 def scatter_kernel(
-    part_ref, in_ref, out_ref, pair, mine, first, middle, second, pair_sem, first_sem, second_sem
+    x_norm_hbm, dproj_hbm, dy_hbm, gated_hbm, in_ref, out_ref,
+    x_norm_ref, dproj_ref, dy_ref, gated_ref, load_sem, x_turned, dy_turned, part, pair, mine, first, middle, second, pair_sem, first_sem, second_sem,
 ):
-    me = lax.axis_index("dp")
-    y, z, c = me // 8, lax.rem(me // 2, 4), lax.rem(me, 2)
+    y, z, c = place()
     steps = (1, 3, 2)
-    peers = [(0, 0, 1)] + [(s, 0, 0) for s in steps] + [(0, s, 0) for s in steps]
-    barrier = pltpu.get_barrier_semaphore()
-    for peer in peers:
-        pl.semaphore_signal(barrier, inc=1, device_id={"dp": chip_at(peer)}, device_id_type=MESH)
-    pl.semaphore_wait(barrier, len(peers))
+    loads = [
+        pltpu.make_async_copy(src, dst, load_sem.at[i])
+        for i, (src, dst) in enumerate(
+            [(x_norm_hbm, x_norm_ref), (dproj_hbm, dproj_ref), (dy_hbm, dy_ref), (gated_hbm, gated_ref)]
+        )
+    ]
+    for load in loads:
+        load.start()
+    greet_all([(0, 0, 1)] + [(s, 0, 0) for s in steps] + [(0, s, 0) for s in steps])
 
     def copy(src, dst, sems, offset):
-        made = pltpu.make_async_remote_copy(
-            src_ref=src,
-            dst_ref=dst,
-            send_sem=sems.at[0],
-            recv_sem=sems.at[1],
-            device_id={"dp": chip_at(offset)},
-            device_id_type=MESH,
-        )
+        made = to_peer(src, dst, sems.at[0], sems.at[1], chip_at(offset))
         made.start()
         return made
 
-    cols = [pl.ds(h * HALF, HALF) for h in range(2)]
-    swaps = [
-        copy(part_ref.at[:, :, 1 - c, :, cols[h]], pair.at[h], pair_sem.at[h], (0, 0, 1)) for h in range(2)
-    ]
-    moves = [[], []]
-    for h in range(2):
-        swaps[h].wait()
-
-        def join(i, carry, h=h):
-            total = part_ref[i, :, c, :, h * HALF : (h + 1) * HALF].astype(F32) + pair[h, i].astype(F32)
-            mine[h, i] = total.astype(BF16)
+    for load in loads:
+        load.wait()
+    x_turned[...] = x_norm_ref[...].T
+
+    def multiply(q):
+        def one(i, carry):
+            rows = pl.ds(pl.multiple_of(i * 256, 256), 256)
+
+            def keep(left, right, start):
+                made = dot(left[rows], right).astype(BF16)
+                width = made.shape[1]
+                part[q, i, :, :, :, start : start + width] = made.reshape(4, 2, CHUNK, width)
+
+            if q < PARTS - 1:
+                keep(x_turned, dproj_ref[:, q * WIDE : (q + 1) * WIDE], 0)
+            else:
+                keep(x_turned, dproj_ref[:, q * WIDE :], 0)
+                keep(dy_turned, gated_ref[...], LAST)
             return carry
 
+        lax.fori_loop(0, 4, one, 0)
+        return copy(part.at[q, :, :, 1 - c], pair.at[q], pair_sem.at[q], (0, 0, 1))
+
+    def move(q, swap):
+        swap.wait()
+
+        def join(i, carry):
+            mine[q, i] = (part[q, i, :, c].astype(F32) + pair[q, i].astype(F32)).astype(BF16)
+            return carry
+
         lax.fori_loop(0, 4, join, 0)
+        moves = []
         for k, s in enumerate(steps):
-            offset = (s, 0, 0) if h == 0 else (0, s, 0)
-            at = lax.rem((z if h else y) + s, 4)
-            src = mine.at[h, :, at] if h else mine.at[h, at]
-            moves[h].append(copy(src, first.at[h, k], first_sem.at[h, k], offset))
-    later = [[], []]
-    for h in range(2):
-        for move in moves[h]:
-            move.wait()
-
-        def add(i, carry, h=h):
-            total = (mine[h, i, z] if h else mine[h, y, i]).astype(F32)
+            along_z = q % 2
+            at = lax.rem((z if along_z else y) + s, 4)
+            src = mine.at[q, :, at] if along_z else mine.at[q, at]
+            moves.append(copy(src, first.at[q, k], first_sem.at[q, k], (0, s, 0) if along_z else (s, 0, 0)))
+        return moves
+
+    swaps, moves, later = [], [], []
+    for q in range(PARTS):
+        if q == PARTS - 1:
+            dy_turned[...] = dy_ref[...].T
+        swaps.append(multiply(q))
+        if q:
+            moves.append(move(q - 1, swaps[q - 1]))
+    moves.append(move(PARTS - 1, swaps[PARTS - 1]))
+    for q in range(PARTS):
+        for made in moves[q]:
+            made.wait()
+        along_z = q % 2
+
+        def add(i, carry, q=q, along_z=along_z):
+            total = (mine[q, i, z] if along_z else mine[q, y, i]).astype(F32)
             for k in range(3):
-                total += first[h, k, i].astype(F32)
-            middle[h, i] = total.astype(BF16)
+                total += first[q, k, i].astype(F32)
+            middle[q, i] = total.astype(BF16)
             return carry
 
         lax.fori_loop(0, 4, add, 0)
+        sent = []
         for k, s in enumerate(steps):
-            offset = (0, s, 0) if h == 0 else (s, 0, 0)
-            at = lax.rem((y if h else z) + s, 4)
-            later[h].append(copy(middle.at[h, at], second.at[h, k], second_sem.at[h, k], offset))
-    for h in range(2):
-        for move in later[h]:
-            move.wait()
-        total = middle[h, y if h else z].astype(F32)
+            at = lax.rem((y if along_z else z) + s, 4)
+            sent.append(
+                copy(middle.at[q, at], second.at[q, k], second_sem.at[q, k], (s, 0, 0) if along_z else (0, s, 0))
+            )
+        later.append(sent)
+    for q in range(PARTS):
+        for made in later[q]:
+            made.wait()
+        total = middle[q, y if q % 2 else z].astype(F32)
         for k in range(3):
-            total += second[h, k].astype(F32)
-        if h == 0:
-            in_ref[:, :HALF] = total
+            total += second[q, k].astype(F32)
+        if q < PARTS - 1:
+            in_ref[:, q * WIDE : (q + 1) * WIDE] = total
         else:
-            in_ref[:, HALF:] = total[:, : 4 * HA - HALF]
-            out_ref[...] = total[:, 4 * HA - HALF :]
-
-
-def summed(part):
+            in_ref[:, q * WIDE :] = total[:, :LAST]
+            out_ref[...] = total[:, LAST:]
+
+
+def summed(x_norm, dproj, dy, gated):
     return pl.pallas_call(
         scatter_kernel,
         out_shape=[
             jax.ShapeDtypeStruct((CHUNK, 4 * HA), F32),
             jax.ShapeDtypeStruct((CHUNK, HA), F32),
         ],
-        in_specs=[VM],
+        in_specs=[ANY] * 4,
         out_specs=[VM, VM],
         scratch_shapes=[
-            pltpu.VMEM((2, 4, 4, CHUNK, HALF), BF16),
-            pltpu.VMEM((2, 4, 4, CHUNK, HALF), BF16),
-            pltpu.VMEM((2, 3, 4, CHUNK, HALF), BF16),
-            pltpu.VMEM((2, 4, CHUNK, HALF), BF16),
-            pltpu.VMEM((2, 3, CHUNK, HALF), BF16),
-            pltpu.SemaphoreType.DMA((2, 2)),
-            pltpu.SemaphoreType.DMA((2, 3, 2)),
-            pltpu.SemaphoreType.DMA((2, 3, 2)),
+            pltpu.VMEM((ROWS, D), BF16),
+            pltpu.VMEM((ROWS, 4 * HA), BF16),
+            pltpu.VMEM((ROWS, D), BF16),
+            pltpu.VMEM((ROWS, HA), BF16),
+            pltpu.SemaphoreType.DMA((4,)),
+            pltpu.VMEM((D, ROWS), BF16),
+            pltpu.VMEM((D, ROWS), BF16),
+            pltpu.VMEM((PARTS, 4, 4, 2, CHUNK, WIDE), BF16),
+            pltpu.VMEM((PARTS, 4, 4, CHUNK, WIDE), BF16),
+            pltpu.VMEM((PARTS, 4, 4, CHUNK, WIDE), BF16),
+            pltpu.VMEM((PARTS, 3, 4, CHUNK, WIDE), BF16),
+            pltpu.VMEM((PARTS, 4, CHUNK, WIDE), BF16),
+            pltpu.VMEM((PARTS, 3, CHUNK, WIDE), BF16),
+            pltpu.SemaphoreType.DMA((PARTS, 2)),
+            pltpu.SemaphoreType.DMA((PARTS, 3, 2)),
+            pltpu.SemaphoreType.DMA((PARTS, 3, 2)),
         ],
         compiler_params=pltpu.CompilerParams(
-            collective_id=1, has_side_effects=True, vmem_limit_bytes=40 << 20
+            collective_id=1, has_side_effects=True, vmem_limit_bytes=60 << 20
         ),
         name="scatter",
-    )(part)
+    )(x_norm, dproj, dy, gated)
 
 
 def body(
@@ -630,8 +671,7 @@
     y, dx, x_norm, dproj, dy, gated = window(
         where, live, embeddings, cotangent, w_in, w_out, fetched
     )
-    part = jnp.concatenate([dot(x_norm, dproj, 0, 0), dot(dy, gated, 0, 0)], axis=1).astype(BF16)
-    grad_in, grad_out = summed(part.reshape(4, 4, 2, CHUNK, 5 * HA))
+    grad_in, grad_out = summed(x_norm, dproj, dy, gated)
     return (y[None], dx[None], grad_in[None], grad_out[None])
 
 

time: 377 us -> 292 us (0.77)
  Pallas kernels: 363 us -> 278 us
  matrix products: 4.02 us -> 0 us
  local copies, waits for them, and re-layouts: 4.36 us -> 8.33 us
    pallas_call x1 -> x0, Pallas kernels: 66.5 us -> none  [fourth(): pl.pallas_call(fourth_kernel, out_shape=jax.ShapeDtypeStruct(got.shape, B...]
    pallas_call x1, Pallas kernels: 110 us -> 95.8 us  [window(): pl.pallas_call(window_kernel, out_shape=[jax.ShapeDtypeStruct((ROWS, D),...]
    dot_general x2 -> x0, matrix products: 4.02 us -> none  [dot(): lax.dot_general(a, b, (((ca,), (cb,)), ((), ())), preferred_element_type=...]
    unnamed x5 -> x9, local copies, waits for them, and re-layouts: 3.43 us -> 7.4 us
where the time goes in v5:
time: 292 us; the launch traced here: 291 us
  Pallas kernels  278 us (95%)
  local copies, waits for them, and re-layouts  8.33 us (3%)
  other arithmetic  3.16 us (1%)
    pallas_call x1, Pallas kernels, exchange(): pl.pallas_call(exchange_kernel, out_shape=[jax.ShapeDtypeStruct((OWNERS /...  153 us
    pallas_call x1, Pallas kernels, window(): pl.pallas_call(window_kernel, out_shape=[jax.ShapeDtypeStruct((ROWS, D),...  95.8 us
    pallas_call x1, Pallas kernels, summed(): pl.pallas_call(scatter_kernel, out_shape=[jax.ShapeDtypeStruct((CHUNK, 4...  29.7 us
    unnamed x9, local copies, waits for them, and re-layouts  7.4 us

profile of v5, /device:TPU:0, one launch (start us, length us, event | category | flops | bytes accessed | tf_op | source)
XLA Modules:
  0.0 291.2 jit_solution(17128977639456193127)
XLA Ops:
  0.6 0.5 broadcast.275
  1.2 1.3 reduce.4
  2.5 0.1 reshape.138
  2.6 0.8 reshape.139
  3.4 0.8 compare_select_fusion.2
  4.1 0.1 reshape.137.live_ref
  4.2 0.0 copy-start
  4.2 0.2 convert_reduce_fusion
  4.4 0.0 copy-start.1
  4.4 0.1 add_reduce_fusion
  4.5 152.8 %exchange.1 = (bf16[16,4,128,1024]{3,2,1,0:T(8,128)(2,1)}, s32[32,1,128]{2,1,0:T(1,128)S(1)}) custom-call(s32[1,128]{1,0:T(1,128)S(1)} %bitcast.10, bf16[16,128,1024]{2,1,0:T(8,128)(2,1)} %bitcast.12), custom_call_target="tpu_custom_call" | custom-call | tf_op jit(solution)/shard_map/exchange/pallas_call | solution.py:168
  157.4 0.7 slice_reduce_fusion
  158.8 0.0 copy-done
  158.8 0.0 copy-done.1
  158.8 95.8 %window.1 = (bf16[256,1024]{1,0:T(8,128)(2,1)}, bf16[256,1024]{1,0:T(8,128)(2,1)}, bf16[256,1024]{1,0:T(8,128)(2,1)}, bf16[256,2048]{1,0:T(8,128)(2,1)}, bf16[25...) custom-call(s32[32]{0:T(128)} %copy-done.1, s32[32]{0:T(128)} %copy-done, bf16[256,1024]{1,0:T(8,128)(2,1)} %x_ref.1, ...), custom_call_target="tpu_custom_call" | custom-call | tf_op jit(solution)/shard_map/window/pallas_call | solution.py:456
  254.6 29.7 %scatter.1 = (f32[32,2048]{1,0:T(8,128)}, f32[32,512]{1,0:T(8,128)}) custom-call(bf16[256,1024]{1,0:T(8,128)(2,1)} %get-tuple-element.37.x_norm_hbm, bf16[256,2048]{1,0:T(8,128)(2,1)} %get-tuple-element.38.dproj_hbm, bf16[256,1024]{1,0:T(8,128)(2,1)} %get-tuple-element.39.dy_hbm, bf16[256,512]{1,0:T(8,128)(2,1)} %get-tuple-element.40.gated_hbm), custom_call_target="tpu_custom_call" | custom-call | tf_op jit(solution)/shard_map/scatter/pallas_call | solution.py:606
  284.3 1.9 copy.21
  286.2 1.9 copy.22
  288.0 1.7 copy.23
  289.7 1.5 copy.24
  (6 shorter events, 0.0 us)
Async XLA Ops:
  4.2 154.6 %copy-start = (s32[32]{0:T(128)}, s32[32]{0:T(128)S(1)}, u32[]{:S(2)}) copy-start(s32[32]{0:T(128)S(1)} %reshape.137.live_ref) | copy-start | bytes 388
  4.4 154.4 %copy-start.1 = (s32[32]{0:T(128)}, s32[32]{0:T(128)S(1)}, u32[]{:S(2)}) copy-start(s32[32]{0:T(128)S(1)} %get-tuple-element.55.where_ref) | copy-start | bytes 388

commit v6 on v5

--- a/solution.py
+++ b/solution.py
@@ -246,10 +246,11 @@
 
 def window_kernel(
     where_ref, live_ref, x_ref, cot_ref, w_in_ref, w_out_ref, fetched_ref,
-    y_ref, dx_ref, x_norm_ref, dproj_ref, dy_ref, gated_ref,
+    made_ref, x_norm_ref, dproj_ref, dy_ref, gated_ref,
     fetched, hist, w_in_t, x_now, x_value, x_rate, act, slope_in, slope, own_weights, mixed, value_ref, rate_ref, dmixed,
     x_arrived, dy_arrived, hist_sem, x_send, x_recv, dy_send, dy_recv,
 ):
+    y_ref, dx_ref = made_ref.at[0], made_ref.at[1]
     section = lax.axis_index("section")
     dp = lax.axis_index("dp")
     after, before = lax.rem(section + 1, 4), lax.rem(section + 3, 4)
@@ -378,11 +379,6 @@
 
         return carry
 
-    lax.fori_loop(0, USERS, forward_user, 0)
-
-    @pl.when(section == 0)
-    def _():
-        turn_w_in()
 
     def backward_user(user, carry):
         rows = user_rows(user)
@@ -435,7 +431,26 @@
 
         return carry
 
-    lax.fori_loop(0, USERS, backward_user, 0)
+    def one_pass(i, carry):
+        last = section == 3
+        user = jnp.where(last, i // 2, lax.rem(i, 2))
+        back = jnp.where(last, lax.rem(i, 2), i // 2)
+
+        @pl.when(back == 0)
+        def _():
+            forward_user(user, 0)
+
+        @pl.when((section == 0) & (i == USERS))
+        def _():
+            turn_w_in()
+
+        @pl.when(back == 1)
+        def _():
+            backward_user(user, 0)
+
+        return carry
+
+    lax.fori_loop(0, 2 * USERS, one_pass, 0)
 
     def finish(user, carry):
         @pl.when(section < 3)
@@ -456,15 +471,14 @@
     return pl.pallas_call(
         window_kernel,
         out_shape=[
-            jax.ShapeDtypeStruct((ROWS, D), BF16),
-            jax.ShapeDtypeStruct((ROWS, D), BF16),
+            jax.ShapeDtypeStruct((2, ROWS, D), BF16),
             jax.ShapeDtypeStruct((ROWS, D), BF16),
             jax.ShapeDtypeStruct((ROWS, 4 * HA), BF16),
             jax.ShapeDtypeStruct((ROWS, D), BF16),
             jax.ShapeDtypeStruct((ROWS, HA), BF16),
         ],
         in_specs=[SM, SM, VM, VM, VM, VM, ANY],
-        out_specs=[VM] * 6,
+        out_specs=[VM] * 5,
         scratch_shapes=[
             pltpu.VMEM(fetched.shape, BF16),
             pltpu.VMEM((USERS * HBLK, EVT, 2 * HA), BF16),
@@ -502,7 +516,7 @@
 
 
 def scatter_kernel(
-    x_norm_hbm, dproj_hbm, dy_hbm, gated_hbm, in_ref, out_ref,
+    x_norm_hbm, dproj_hbm, dy_hbm, gated_hbm, sum_ref,
     x_norm_ref, dproj_ref, dy_ref, gated_ref, load_sem, x_turned, dy_turned, part, pair, mine, first, middle, second, pair_sem, first_sem, second_sem,
 ):
     y, z, c = place()
@@ -595,22 +609,15 @@
         total = middle[q, y if q % 2 else z].astype(F32)
         for k in range(3):
             total += second[q, k].astype(F32)
-        if q < PARTS - 1:
-            in_ref[:, q * WIDE : (q + 1) * WIDE] = total
-        else:
-            in_ref[:, q * WIDE :] = total[:, :LAST]
-            out_ref[...] = total[:, LAST:]
+        sum_ref[:, q * WIDE : (q + 1) * WIDE] = total
 
 
 def summed(x_norm, dproj, dy, gated):
     return pl.pallas_call(
         scatter_kernel,
-        out_shape=[
-            jax.ShapeDtypeStruct((CHUNK, 4 * HA), F32),
-            jax.ShapeDtypeStruct((CHUNK, HA), F32),
-        ],
+        out_shape=jax.ShapeDtypeStruct((CHUNK, 5 * HA), F32),
         in_specs=[ANY] * 4,
-        out_specs=[VM, VM],
+        out_specs=VM,
         scratch_shapes=[
             pltpu.VMEM((ROWS, D), BF16),
             pltpu.VMEM((ROWS, 4 * HA), BF16),
@@ -668,11 +675,11 @@
         jnp.max(asked[:, 0, 127]) > 0, lambda g: fourth(asked, cache, g), lambda g: g, got
     )
     fetched = got.reshape(OWNERS // 2 * SLOTS, EVT, 2 * HA)
-    y, dx, x_norm, dproj, dy, gated = window(
+    made, x_norm, dproj, dy, gated = window(
         where, live, embeddings, cotangent, w_in, w_out, fetched
     )
-    grad_in, grad_out = summed(x_norm, dproj, dy, gated)
-    return (y[None], dx[None], grad_in[None], grad_out[None])
+    grads = summed(x_norm, dproj, dy, gated)[None]
+    return (made[:1], made[1:], grads[:, :, : 4 * HA], grads[:, :, 4 * HA :])
 
 
 def solution(mesh):

time: 292 us -> 286 us (0.979)
  Pallas kernels: 278 us -> 274 us
    unnamed x9 -> x5, local copies, waits for them, and re-layouts: 7.4 us -> 0.52 us
    slice x0 -> x3, local copies, waits for them, and re-layouts: none -> 5.38 us  [body(): return (made[:1], made[1:], grads[:, :, :4 * HA], grads[:, :, 4 * HA:])]
    pallas_call x2, Pallas kernels: 125 us -> 121 us  [the longest x1 87.8 us: window(): pl.pallas_call(window_kernel, out_shape=[jax.ShapeDtypeStruct((2, ROWS, D...]
where the time goes in v6:
time: 286 us; the launch traced here: 285 us
  Pallas kernels  274 us (96%)
  local copies, waits for them, and re-layouts  6.83 us (2%)
  other arithmetic  3.16 us (1%)
    pallas_call x1, Pallas kernels, exchange(): pl.pallas_call(exchange_kernel, out_shape=[jax.ShapeDtypeStruct((OWNERS /...  153 us
    pallas_call x1, Pallas kernels, window(): pl.pallas_call(window_kernel, out_shape=[jax.ShapeDtypeStruct((2, ROWS, D...  87.8 us
    pallas_call x1, Pallas kernels, summed(): pl.pallas_call(scatter_kernel, out_shape=jax.ShapeDtypeStruct((CHUNK, 5 *...  33.3 us

profile of v6, /device:TPU:0, one launch (start us, length us, event | category | flops | bytes accessed | tf_op | source)
XLA Modules:
  0.0 285.4 jit_solution(9593177841398385415)
XLA Ops:
  0.6 0.5 broadcast.275
  1.2 1.3 reduce.4
  2.5 0.1 reshape.138
  2.6 0.8 reshape.139
  3.4 0.8 compare_select_fusion.2
  4.1 0.1 reshape.137.live_ref
  4.2 0.0 copy-start
  4.2 0.2 convert_reduce_fusion
  4.4 0.0 copy-start.1
  4.4 0.1 add_reduce_fusion
  4.5 152.8 %exchange.1 = (bf16[16,4,128,1024]{3,2,1,0:T(8,128)(2,1)}, s32[32,1,128]{2,1,0:T(1,128)S(1)}) custom-call(s32[1,128]{1,0:T(1,128)S(1)} %bitcast.7, bf16[16,128,1024]{2,1,0:T(8,128)(2,1)} %bitcast.9), custom_call_target="tpu_custom_call" | custom-call | tf_op jit(solution)/shard_map/exchange/pallas_call | solution.py:168
  157.4 0.7 slice_reduce_fusion
  158.8 0.0 copy-done
  158.8 0.0 copy-done.1
  158.8 87.8 %window.1 = (bf16[2,256,1024]{2,1,0:T(8,128)(2,1)}, bf16[256,1024]{1,0:T(8,128)(2,1)}, bf16[256,2048]{1,0:T(8,128)(2,1)}, bf16[256,1024]{1,0:T(8,128)(2,1)}, bf16[256,512]{1,0:T(8,128)(2,1)}) custom-call(s32[32]{0:T(128)} %copy-done.1, s32[32]{0:T(128)} %copy-done, bf16[256,1024]{1,0:T(8,128)(2,1)} %x_ref.1, bf16[256,1024]{1,0:T(8,128)(2,1)} %cot_ref.1, ...), custom_call_target="tpu_custom_call" | custom-call | tf_op jit(solution)/shard_map/window/pallas_call | solution.py:471
  246.6 2.2 fusion.2
  248.9 33.3 %scatter.1 = f32[32,2560]{1,0:T(8,128)} custom-call(bf16[256,1024]{1,0:T(8,128)(2,1)} %get-tuple-element.33.x_norm_hbm, bf16[256,2048]{1,0:T(8,128)(2,1)} %get-tuple-element.34.dproj_hbm, bf16[256,1024]{1,0:T(8,128)(2,1)} %get-tuple-element.35.dy_hbm, bf16[256,512]{1,0:T(8,128)(2,1)} %get-tuple-element.36.gated_hbm), custom_call_target="tpu_custom_call" | custom-call | tf_op jit(solution)/shard_map/scatter/pallas_call | solution.py:616
  282.2 1.5 slice.21
  283.7 1.7 slice.20
  (6 shorter events, 0.0 us)
Async XLA Ops:
  4.2 154.6 %copy-start = (s32[32]{0:T(128)}, s32[32]{0:T(128)S(1)}, u32[]{:S(2)}) copy-start(s32[32]{0:T(128)S(1)} %reshape.137.live_ref) | copy-start | bytes 388
  4.4 154.4 %copy-start.1 = (s32[32]{0:T(128)}, s32[32]{0:T(128)S(1)}, u32[]{:S(2)}) copy-start(s32[32]{0:T(128)S(1)} %get-tuple-element.51.where_ref) | copy-start | bytes 388
